TPU v7x, 1024 devices: a whole 4x8x16 slice. The times are simulated.
1024 devices in a mesh: row: 16 (over y, core), col: 64 (over x, z).
Axes of the slice: x: 4, y: 8, z: 16, core: 2. Of those that a mesh axis runs over, the one named last changes fastest.
Arguments:
- obj_slices: float32 [2, 2, 2048, 8192], P(None, None, 'row', 'col'), may hold values from -5 to 5
- probe_wave: float32 [2, 128, 128], replicated, may hold values from -5 to 5
- prop_phase: float32 [128, 128], replicated, may hold values from -3.140625 to 3.140625
- measured: float32 [16, 64, 2, 128, 128], P('row', 'col'), may hold values from 0 to 2
- positions: int32 [16, 64, 2, 2], P('row', 'col'), may hold values from 0 to 8064, as said below
- counts: int32 [16, 64], P('row', 'col'), may hold values from 0 to 2, as said below
Outputs:
- gradient: float32 [2, 2, 2048, 8192], P(None, None, 'row', 'col')
Inputs may be any that keep to these rules, and one draw needn't show every extreme that they name: `positions`: for the device at mesh row r and column c, each window starts at row min(max(r * 128 - 64 + u, 0), 1920) and column min(max(c * 128 - 64 + v, 0), 8064) for some 0 <= u < 128, 0 <= v < 128; dimension 2 holds the row, then the column. `counts`: live slots are the first ones of a device. The devices at mesh columns 2 * i and 2 * i + 1 of one mesh row hold at most 2 live slots together, and in every draw some device holds 2.
All inputs are finite; a program needn't handle non-finite values.
Results may differ from a plain program's by a relative error of at most 0.0003.
Values sent between devices are 32-bit elements; how exact they have to be, the bound alone decides.
No kernel may reach another device: no remote copies, remote signals or barrier semaphores. Data moves between devices by JAX's collectives and lax.ppermute only.
A program may use at most 32 MiB of HBM per device.

v0:
```python
import math

import jax
import jax.numpy as jnp
from jax import lax
from jax.sharding import PartitionSpec as P


def extended_2(block, sides, width):
    for axis, dim in sides:
        count = lax.axis_size(axis)
        forward = [(i, i + 1) for i in range(count - 1)]
        backward = [(target, source) for source, target in forward]
        low = lax.ppermute(
            lax.slice_in_dim(block, block.shape[dim] - width, None, axis=dim), axis, forward
        )
        high = lax.ppermute(lax.slice_in_dim(block, 0, width, axis=dim), axis, backward)
        block = jnp.concatenate([low, block, high], axis=dim)
    return block


def dft_tables(sequence_length):
    index_row = jnp.arange(sequence_length, dtype=jnp.int32)
    product = index_row[:, None] * index_row[None, :] % sequence_length
    angles = product.astype(jnp.float32) * (-2.0 * math.pi / sequence_length)
    factor = 1.0 / math.sqrt(sequence_length)
    return (jnp.cos(angles) * factor, jnp.sin(angles) * factor)


def apply_left(matrix, batch):
    return jnp.einsum("kn,bnm->bkm", matrix, batch, precision=lax.Precision.HIGHEST)


def apply_right(batch, matrix):
    return jnp.einsum("bkn,nm->bkm", batch, matrix, precision=lax.Precision.HIGHEST)


def transform(real_part, imag_part, w_real, w_imag):
    left_re = apply_left(w_real, real_part) - apply_left(w_imag, imag_part)
    left_im = apply_left(w_real, imag_part) + apply_left(w_imag, real_part)
    out_re = apply_right(left_re, w_real) - apply_right(left_im, w_imag)
    out_im = apply_right(left_re, w_imag) + apply_right(left_im, w_real)
    return (out_re, out_im)


def batch_loss(patches, targets, probe_wave, kernel_re, kernel_im, w_real, w_imag):
    wave_re = jnp.broadcast_to(probe_wave[0], targets.shape)
    wave_im = jnp.broadcast_to(probe_wave[1], targets.shape)
    slab_count = patches.shape[2]
    for slab_index in range(slab_count):
        trans_re = patches[:, 0, slab_index]
        trans_im = patches[:, 1, slab_index]
        wave_re, wave_im = (
            trans_re * wave_re - trans_im * wave_im,
            trans_re * wave_im + trans_im * wave_re,
        )
        if slab_index + 1 < slab_count:
            spec_re, spec_im = transform(wave_re, wave_im, w_real, w_imag)
            spec_re, spec_im = (
                kernel_re * spec_re - kernel_im * spec_im,
                kernel_re * spec_im + kernel_im * spec_re,
            )
            wave_re, wave_im = transform(spec_re, spec_im, w_real, -w_imag)
    far_re, far_im = transform(wave_re, wave_im, w_real, w_imag)
    misfit = far_re * far_re + far_im * far_im - targets
    return 0.25 * jnp.sum(misfit * misfit)


def window_grads(patches, targets, probe_wave, kernel_re, kernel_im, w_real, w_imag):
    return jax.grad(batch_loss)(patches, targets, probe_wave, kernel_re, kernel_im, w_real, w_imag)


def fold_axis(source, axis_dim, inner_len, margin):
    middle = lax.slice_in_dim(source, 2 * margin, 2 * margin + inner_len, axis=axis_dim)
    leading = lax.slice_in_dim(source, 0, margin, axis=axis_dim)
    trailing = lax.slice_in_dim(
        source, inner_len + 3 * margin, inner_len + 4 * margin, axis=axis_dim
    )
    pad_leading = [(0, 0)] * source.ndim
    pad_leading[axis_dim] = (0, inner_len - margin)
    pad_trailing = [(0, 0)] * source.ndim
    pad_trailing[axis_dim] = (inner_len - margin, 0)
    return middle + jnp.pad(leading, pad_leading) + jnp.pad(trailing, pad_trailing)


def per_device(obj_slices, probe_wave, prop_phase, measured, positions, counts):
    tile_rows = obj_slices.shape[2]
    tile_cols = obj_slices.shape[3]
    sequence_length = probe_wave.shape[1]
    margin = sequence_length // 2
    slot_count = positions.shape[3]
    w_real, w_imag = dft_tables(sequence_length)
    kernel_re = jnp.cos(prop_phase)
    kernel_im = jnp.sin(prop_phase)
    extended = extended_2(obj_slices, (("row", 2), ("col", 3)), margin)
    local_y = positions[0, 0, 0] - lax.axis_index("row") * tile_rows + margin
    local_x = positions[0, 0, 1] - lax.axis_index("col") * tile_cols + margin
    zero_index = jnp.zeros((), jnp.int32)
    slab_count = extended.shape[1]

    def cut_patch(start_y, start_x):
        return lax.dynamic_slice(
            extended,
            (zero_index, zero_index, start_y, start_x),
            (2, slab_count, sequence_length, sequence_length),
        )

    patches = jax.vmap(cut_patch)(local_y, local_x)
    targets = measured[0, 0]
    loaded = counts[0, 0]
    slot_ids = jnp.arange(slot_count, dtype=jnp.int32)
    gradients = window_grads(patches, targets, probe_wave, kernel_re, kernel_im, w_real, w_imag)
    live_mask = (slot_ids < loaded).astype(jnp.float32)
    gradients = gradients * live_mask[:, None, None, None, None]

    def add_patch(slot_index, buffer):
        anchor = (zero_index, zero_index, local_y[slot_index], local_x[slot_index])
        current = lax.dynamic_slice(
            buffer, anchor, (2, slab_count, sequence_length, sequence_length)
        )
        return lax.dynamic_update_slice(buffer, current + gradients[slot_index], anchor)

    accum = lax.fori_loop(0, slot_count, add_patch, jnp.zeros(extended.shape, jnp.float32))
    spread = extended_2(accum, (("row", 2), ("col", 3)), margin)
    folded = fold_axis(spread, 2, tile_rows, margin)
    folded = fold_axis(folded, 3, tile_cols, margin)
    return folded


def solution(mesh):
    placed = (
        P(None, None, "row", "col"),
        P(),
        P(),
        P("row", "col", None, None, None),
        P("row", "col", None, None),
        P("row", "col"),
    )
    return jax.shard_map(
        per_device,
        mesh=mesh,
        in_specs=placed,
        out_specs=P(None, None, "row", "col"),
        check_vma=False,
    )
```

profile of v0, /device:TPU:15, one launch (start us, length us, event | category | flops | bytes accessed | tf_op | source)
XLA Modules:
  0.0 125.5 jit_solution(10038741409020852467)
XLA Ops:
  0.0 1.0 fusion.369
  1.0 2.6 %collective-permute-start.1 = (f32[2,2,64,128]{3,2,1,0:T(8,128)S(1)}, f32[2,2,64,128]{3,2,1,0:T(8,128)S(1)}, u32[]{:S(2)}, u32[]{:S(2)}) collective-permute-start(f32[2,2,64,128]{3,2,1,0:T(8,128)S(1)} %get-tuple-element.154), channel_id=1, source_target_pairs={{64,0},{128,64},{192,128},{256,192},{320,256},{384,320},{448,384},... | collective-permute-start | bytes 393224 | tf_op jit(solution)/shard_map/ppermute | solution.py:17
  3.6 3.1 %collective-permute-start = (f32[2,2,64,128]{3,2,1,0:T(8,128)S(1)}, f32[2,2,64,128]{3,2,1,0:T(8,128)S(1)}, u32[]{:S(2)}, u32[]{:S(2)}) collective-permute-start(f32[2,2,64,128]{3,2,1,0:T(8,128)S(1)} %get-tuple-element.155), channel_id=1, source_target_pairs={{0,64},{64,128},{128,192},{192,256},{256,320},{320,384},{384,448},... | collective-permute-start | bytes 393224 | tf_op jit(solution)/shard_map/ppermute | solution.py:14
  9.1 0.9 slice_bitcast_fusion.1
  10.1 1.0 constant_dynamic-update-slice_fusion.1
  11.3 4.0 %collective-permute-start.2 = (f32[2,2,256,64]{3,2,1,0:T(8,128)S(1)}, f32[2,2,256,64]{3,2,1,0:T(8,128)S(1)}, u32[]{:S(2)}, u32[]{:S(2)}) collective-permute-start(f32[2,2,256,64]{3,2,1,0:T(8,128)S(1)} %get-tuple-element.148), channel_id=1, source_target_pairs={{0,1},{1,2},{2,3},{3,4},{4,5},{5,6},{6,7},{7,8},{8,9},{9,10},{10,1... | collective-permute-start | bytes 786440 | tf_op jit(solution)/shard_map/ppermute | solution.py:14
  15.3 16.1 %collective-permute-start.3 = (f32[2,2,256,64]{3,2,1,0:T(8,128)S(1)}, f32[2,2,256,64]{3,2,1,0:T(8,128)S(1)}, u32[]{:S(2)}, u32[]{:S(2)}) collective-permute-start(f32[2,2,256,64]{3,2,1,0:T(8,128)S(1)} %get-tuple-element.149), channel_id=1, source_target_pairs={{1,0},{2,1},{3,2},{4,3},{5,4},{6,5},{7,6},{8,7},{9,8},{10,9},{11,1... | collective-permute-start | bytes 786440 | tf_op jit(solution)/shard_map/ppermute | solution.py:17
  31.7 10.2 %collective-permute-done.2 = f32[2,2,256,64]{3,2,1,0:T(8,128)S(1)} collective-permute-done((f32[2,2,256,64]{3,2,1,0:T(8,128)S(1)}, f32[2,2,256,64]{3,2,1,0:T(8,128)S(1)}, u32[]{:S(2)}, u32[]{:S(2)}) %collective-permute-start.2) | collective-permute-done | bytes 262176 | tf_op jit(solution)/shard_map/ppermute | solution.py:14
  42.0 0.9 collective-permute-done.3
  43.3 4.3 %while.15 = (s32[]{:T(128)}, f32[2,2,256,256]{3,2,1,0:T(8,128)S(1)}, s32[2,4]{1,0:T(2,128)S(1)}, f32[2,2,2,128,128]{4,3,0,2,1:T(8,128)S(1)}, s32[]{:T(128)}) while((s32[]{:T(128)}, f32[2,2,256,256]{3,2,1,0:T(8,128)S(1)}, s32[2,4]{1,0:T(2,128)S(1)}, f32[2,2,2,128,128]{4,3,0,2,1:T(8,128)S(1)}, s32[]{:T(128)}) %tuple.59), condition=%wide.while_cond, body=%wide.while_body.sunk | while | flops 2 | bytes 524421 | solution.py:102
  44.0 1.5 %bitcast_dynamic-update-slice_fusion.2 = f32[2,2,2,128,128]{4,3,0,2,1:T(8,128)S(1)} fusion(f32[2,2,2,128,128]{4,3,0,2,1:T(8,128)S(1)} %get-tuple-element.233, s32[]{:T(128)S(6)} %copy.191, f32[2,2,256,256]{3,2,1,0:T(8,128)S(1)} %get-tuple-element.236, s32[]{:T(128)} %bitcast.284, s32[]{:T(128)} %bitcast.285), kind=kLoop, calls=%fused_computation.2.clone.1 | loop fusion | bytes 524300 | tf_op jit(solution)/shard_map/vmap()/gather
  46.2 1.5 %bitcast_dynamic-update-slice_fusion.2 = f32[2,2,2,128,128]{4,3,0,2,1:T(8,128)S(1)} fusion(f32[2,2,2,128,128]{4,3,0,2,1:T(8,128)S(1)} %get-tuple-element.233, s32[]{:T(128)S(6)} %copy.191, f32[2,2,256,256]{3,2,1,0:T(8,128)S(1)} %get-tuple-element.236, s32[]{:T(128)} %bitcast.284, s32[]{:T(128)} %bitcast.285), kind=kLoop, calls=%fused_computation.2.clone.1 | loop fusion | bytes 524300 | tf_op jit(solution)/shard_map/vmap()/gather
  74.9 17.4 %while.14 = (s32[]{:T(128)}, f32[2,2,256,256]{2,3,1,0:T(8,128)S(1)}, s32[2]{0:T(128)S(1)}, s32[2]{0:T(128)S(1)}, f32[2,2,2,128,128]{4,3,0,2,1:T(8,128)S(1)}, /*index=5*/s32[]{:T(128)}, s32[]{:T(128)}, s32[]{:T(128)}) while((s32[]{:T(128)}, f32[2,2,256,256]{2,3,1,0:T(8,128)S(1)}, s32[2]{0:T(128)S(1)}, s32[2]{0:T(128)S(1)}, ...), condition=%wide.region_1.2_spmd, body=%wide.region_0.1_spmd.sunk | while | flops 65544 | bytes 2883785 | solution.py:123
  80.3 3.3 %dynamic_update_slice.8 = f32[2,2,256,256]{2,3,1,0:T(8,128)S(1)} dynamic-update-slice(f32[2,2,256,256]{2,3,1,0:T(8,128)S(1)} %get-tuple-element.249, f32[2,2,128,128]{2,3,1,0:T(8,128)S(1)} %copy.184, s32[]{:T(128)} %constant.61.clone.1..sunk, s32[]{:T(128)} %constant.61.clone.1..sunk, s32[]{:T(128)S(6)} %select_n.310, s32[]{:T(128)S(6)} %select_n.311) | dynamic-update-slice | bytes 524292 | tf_op jit(solution)/shard_map/while/body/eval_jaxpr/dynamic_update_slice | solution.py:121
  89.1 3.3 %dynamic_update_slice.8 = f32[2,2,256,256]{2,3,1,0:T(8,128)S(1)} dynamic-update-slice(f32[2,2,256,256]{2,3,1,0:T(8,128)S(1)} %get-tuple-element.249, f32[2,2,128,128]{2,3,1,0:T(8,128)S(1)} %copy.184, s32[]{:T(128)} %constant.61.clone.1..sunk, s32[]{:T(128)} %constant.61.clone.1..sunk, s32[]{:T(128)S(6)} %select_n.310, s32[]{:T(128)S(6)} %select_n.311) | dynamic-update-slice | bytes 524292 | tf_op jit(solution)/shard_map/while/body/eval_jaxpr/dynamic_update_slice | solution.py:121
  92.5 3.7 %collective-permute-start.4 = (f32[2,2,64,256]{2,3,1,0:T(8,128)S(1)}, f32[2,2,64,256]{2,3,1,0:T(8,128)S(1)}, u32[]{:S(2)}, u32[]{:S(2)}) collective-permute-start(f32[2,2,64,256]{2,3,1,0:T(8,128)S(1)} %get-tuple-element.140), channel_id=1, source_target_pairs={{0,64},{64,128},{128,192},{192,256},{256,320},{320,384},{384,448},... | collective-permute-start | bytes 786440 | tf_op jit(solution)/shard_map/ppermute | solution.py:14
  96.2 1.9 %collective-permute-start.5 = (f32[2,2,64,256]{2,3,1,0:T(8,128)S(1)}, f32[2,2,64,256]{2,3,1,0:T(8,128)S(1)}, u32[]{:S(2)}, u32[]{:S(2)}) collective-permute-start(f32[2,2,64,256]{2,3,1,0:T(8,128)S(1)} %get-tuple-element.141), channel_id=1, source_target_pairs={{64,0},{128,64},{192,128},{256,192},{320,256},{384,320},{448,384},... | collective-permute-start | bytes 786440 | tf_op jit(solution)/shard_map/ppermute | solution.py:17
  98.1 4.2 %collective-permute-done.4 = f32[2,2,64,256]{2,3,1,0:T(8,128)S(1)} collective-permute-done((f32[2,2,64,256]{2,3,1,0:T(8,128)S(1)}, f32[2,2,64,256]{2,3,1,0:T(8,128)S(1)}, u32[]{:S(2)}, u32[]{:S(2)}) %collective-permute-start.4) | collective-permute-done | bytes 262176 | tf_op jit(solution)/shard_map/ppermute | solution.py:14
  102.3 4.4 %collective-permute-done.5 = f32[2,2,64,256]{2,3,1,0:T(8,128)S(1)} collective-permute-done((f32[2,2,64,256]{2,3,1,0:T(8,128)S(1)}, f32[2,2,64,256]{2,3,1,0:T(8,128)S(1)}, u32[]{:S(2)}, u32[]{:S(2)}) %collective-permute-start.5) | collective-permute-done | bytes 262176 | tf_op jit(solution)/shard_map/ppermute | solution.py:17
  107.0 1.9 %collective-permute-start.6 = (f32[2,2,384,64]{2,3,1,0:T(8,128)S(1)}, f32[2,2,384,64]{2,3,1,0:T(8,128)S(1)}, u32[]{:S(2)}, u32[]{:S(2)}) collective-permute-start(f32[2,2,384,64]{2,3,1,0:T(8,128)S(1)} %get-tuple-element.138), channel_id=1, source_target_pairs={{0,1},{1,2},{2,3},{3,4},{4,5},{5,6},{6,7},{7,8},{8,9},{9,10},{10,1... | collective-permute-start | bytes 1179656 | tf_op jit(solution)/shard_map/ppermute | solution.py:14
  109.0 6.2 %collective-permute-start.7 = (f32[2,2,384,64]{2,3,1,0:T(8,128)S(1)}, f32[2,2,384,64]{2,3,1,0:T(8,128)S(1)}, u32[]{:S(2)}, u32[]{:S(2)}) collective-permute-start(f32[2,2,384,64]{2,3,1,0:T(8,128)S(1)} %get-tuple-element.139), channel_id=1, source_target_pairs={{1,0},{2,1},{3,2},{4,3},{5,4},{6,5},{7,6},{8,7},{9,8},{10,9},{11,1... | collective-permute-start | bytes 1179656 | tf_op jit(solution)/shard_map/ppermute | solution.py:17
  115.2 6.4 %collective-permute-done.6 = f32[2,2,384,64]{2,3,1,0:T(8,128)S(1)} collective-permute-done((f32[2,2,384,64]{2,3,1,0:T(8,128)S(1)}, f32[2,2,384,64]{2,3,1,0:T(8,128)S(1)}, u32[]{:S(2)}, u32[]{:S(2)}) %collective-permute-start.6) | collective-permute-done | bytes 393248 | tf_op jit(solution)/shard_map/ppermute | solution.py:14
  121.6 1.8 %collective-permute-done.7 = f32[2,2,384,64]{2,3,1,0:T(8,128)S(1)} collective-permute-done((f32[2,2,384,64]{2,3,1,0:T(8,128)S(1)}, f32[2,2,384,64]{2,3,1,0:T(8,128)S(1)}, u32[]{:S(2)}, u32[]{:S(2)}) %collective-permute-start.7) | collective-permute-done | bytes 393248 | tf_op jit(solution)/shard_map/ppermute | solution.py:17
  124.6 0.8 copy.120
  (95 shorter events, 36.0 us)
Async XLA Ops:
  0.0 31.5 %copy-start.1 = (f32[128,128]{1,0:T(8,128)S(1)}, f32[128,128]{1,0:T(8,128)}, u32[]{:S(2)}) copy-start(f32[128,128]{1,0:T(8,128)} %param.10) | copy-start | bytes 196612
  1.0 10.0 %collective-permute-start.1 = (f32[2,2,64,128]{3,2,1,0:T(8,128)S(1)}, f32[2,2,64,128]{3,2,1,0:T(8,128)S(1)}, u32[]{:S(2)}, u32[]{:S(2)}) collective-permute-start(f32[2,2,64,128]{3,2,1,0:T(8,128)S(1)} %get-tuple-element.154), channel_id=1, source_target_pairs={{64,0},{128,64},{192,128},{256,192},{320,256},{384,320},{448,384},... | collective-permute-start | bytes 393224 | tf_op jit(solution)/shard_map/ppermute | solution.py:17
  3.6 6.5 %collective-permute-start = (f32[2,2,64,128]{3,2,1,0:T(8,128)S(1)}, f32[2,2,64,128]{3,2,1,0:T(8,128)S(1)}, u32[]{:S(2)}, u32[]{:S(2)}) collective-permute-start(f32[2,2,64,128]{3,2,1,0:T(8,128)S(1)} %get-tuple-element.155), channel_id=1, source_target_pairs={{0,64},{64,128},{128,192},{192,256},{256,320},{320,384},{384,448},... | collective-permute-start | bytes 393224 | tf_op jit(solution)/shard_map/ppermute | solution.py:14
  11.3 30.7 %collective-permute-start.2 = (f32[2,2,256,64]{3,2,1,0:T(8,128)S(1)}, f32[2,2,256,64]{3,2,1,0:T(8,128)S(1)}, u32[]{:S(2)}, u32[]{:S(2)}) collective-permute-start(f32[2,2,256,64]{3,2,1,0:T(8,128)S(1)} %get-tuple-element.148), channel_id=1, source_target_pairs={{0,1},{1,2},{2,3},{3,4},{4,5},{5,6},{6,7},{7,8},{8,9},{9,10},{10,1... | collective-permute-start | bytes 786440 | tf_op jit(solution)/shard_map/ppermute | solution.py:14
  15.3 27.6 %collective-permute-start.3 = (f32[2,2,256,64]{3,2,1,0:T(8,128)S(1)}, f32[2,2,256,64]{3,2,1,0:T(8,128)S(1)}, u32[]{:S(2)}, u32[]{:S(2)}) collective-permute-start(f32[2,2,256,64]{3,2,1,0:T(8,128)S(1)} %get-tuple-element.149), channel_id=1, source_target_pairs={{1,0},{2,1},{3,2},{4,3},{5,4},{6,5},{7,6},{8,7},{9,8},{10,9},{11,1... | collective-permute-start | bytes 786440 | tf_op jit(solution)/shard_map/ppermute | solution.py:17
  55.0 6.4 %copy-start = (f32[1,1,2,128,128]{4,3,2,1,0:T(8,128)S(1)}, f32[1,1,2,128,128]{4,3,2,1,0:T(8,128)}, u32[]{:S(2)}) copy-start(f32[1,1,2,128,128]{4,3,2,1,0:T(8,128)} %param.11) | copy-start | bytes 393220
  92.5 9.8 %collective-permute-start.4 = (f32[2,2,64,256]{2,3,1,0:T(8,128)S(1)}, f32[2,2,64,256]{2,3,1,0:T(8,128)S(1)}, u32[]{:S(2)}, u32[]{:S(2)}) collective-permute-start(f32[2,2,64,256]{2,3,1,0:T(8,128)S(1)} %get-tuple-element.140), channel_id=1, source_target_pairs={{0,64},{64,128},{128,192},{192,256},{256,320},{320,384},{384,448},... | collective-permute-start | bytes 786440 | tf_op jit(solution)/shard_map/ppermute | solution.py:14
  96.2 10.5 %collective-permute-start.5 = (f32[2,2,64,256]{2,3,1,0:T(8,128)S(1)}, f32[2,2,64,256]{2,3,1,0:T(8,128)S(1)}, u32[]{:S(2)}, u32[]{:S(2)}) collective-permute-start(f32[2,2,64,256]{2,3,1,0:T(8,128)S(1)} %get-tuple-element.141), channel_id=1, source_target_pairs={{64,0},{128,64},{192,128},{256,192},{320,256},{384,320},{448,384},... | collective-permute-start | bytes 786440 | tf_op jit(solution)/shard_map/ppermute | solution.py:17
  107.0 14.5 %collective-permute-start.6 = (f32[2,2,384,64]{2,3,1,0:T(8,128)S(1)}, f32[2,2,384,64]{2,3,1,0:T(8,128)S(1)}, u32[]{:S(2)}, u32[]{:S(2)}) collective-permute-start(f32[2,2,384,64]{2,3,1,0:T(8,128)S(1)} %get-tuple-element.138), channel_id=1, source_target_pairs={{0,1},{1,2},{2,3},{3,4},{4,5},{5,6},{6,7},{7,8},{8,9},{9,10},{10,1... | collective-permute-start | bytes 1179656 | tf_op jit(solution)/shard_map/ppermute | solution.py:14
  109.0 15.3 %copy-start.2 = (pred[128]{0:T(512)(128)(4,1)S(1)}, pred[128]{0:T(512)(128)(4,1)}, u32[]{:S(2)}) copy-start(pred[128]{0:T(512)(128)(4,1)} %constant.73.clone.1) | copy-start | bytes 388
  109.0 14.4 %collective-permute-start.7 = (f32[2,2,384,64]{2,3,1,0:T(8,128)S(1)}, f32[2,2,384,64]{2,3,1,0:T(8,128)S(1)}, u32[]{:S(2)}, u32[]{:S(2)}) collective-permute-start(f32[2,2,384,64]{2,3,1,0:T(8,128)S(1)} %get-tuple-element.139), channel_id=1, source_target_pairs={{1,0},{2,1},{3,2},{4,3},{5,4},{6,5},{7,6},{8,7},{9,8},{10,9},{11,1... | collective-permute-start | bytes 1179656 | tf_op jit(solution)/shard_map/ppermute | solution.py:17
where the time goes:
time: 126 us; the launch traced here: 125 us
  starting transfers between devices  39.5 us (31%)
  waiting for transfers between devices  27.9 us (22%)
  matrix products  26.4 us (21%)
  local copies, waits for them, and re-layouts  19.1 us (15%)
  loops' own time  7.68 us (6%)
  other arithmetic  3.58 us (3%)
  between operations  1.26 us (1%)
    ppermute x4, starting transfers between devices, extended_2(): lax.ppermute(lax.slice_in_dim(block, 0, width, axis=dim), axis, backward)  26.8 us
    ppermute x4, waiting for transfers between devices, extended_2(): lax.ppermute(lax.slice_in_dim(block, block.shape[dim] - width, None, axis...  20.8 us
    dot_general x24, matrix products, apply_left(): jnp.einsum('kn,bnm->bkm', matrix, batch, precision=lax.Precision.HIGHEST)  13.4 us
    dot_general x24, matrix products, apply_right(): jnp.einsum('bkn,nm->bkm', batch, matrix, precision=lax.Precision.HIGHEST)  13.1 us
    ppermute x4, starting transfers between devices, extended_2(): lax.ppermute(lax.slice_in_dim(block, block.shape[dim] - width, None, axis...  12.7 us
    another operation x1, loops' own time, per_device(): lax.fori_loop(0, slot_count, add_patch, jnp.zeros(extended.shape, jnp.flo...  7.62 us
    ppermute x4, waiting for transfers between devices, extended_2(): lax.ppermute(lax.slice_in_dim(block, 0, width, axis=dim), axis, backward)  7.07 us
    dynamic_update_slice x4, local copies, waits for them, and re-layouts, add_patch(): lax.dynamic_update_slice(buffer, current + gradients[slot_index], anchor)  6.77 us
  transfers between devices with their start and end apart: 8, of which 6 were waited for; matrix products, arithmetic and copies ran while one was open for 3% of the time, Pallas kernels for 0%

commit v1 on v0

v1 whole, which is shorter than its diff:
```python
import math

import jax
import jax.numpy as jnp
import numpy as np
from jax import lax
from jax.experimental import pallas as pl
from jax.experimental.pallas import tpu as pltpu
from jax.sharding import PartitionSpec as P

N = 128
H = N // 2
F32 = jnp.float32
BF16 = jnp.bfloat16
VMEM = pl.BlockSpec(memory_space=pltpu.VMEM)
SMEM = pl.BlockSpec(memory_space=pltpu.SMEM)


def dft_tables():
    index = np.arange(N)
    angle = (index[:, None] * index[None, :] % N) * (-2.0 * math.pi / N)
    re, im = np.cos(angle) / math.sqrt(N), np.sin(angle) / math.sqrt(N)
    table = np.block([[re, im], [-im, re]]).astype(np.float32)
    out = []
    for one in (table, table.T):
        high = one.astype(jnp.bfloat16)
        out += [high, (one - high.astype(np.float32)).astype(jnp.bfloat16)]
    return np.stack(out)


def swap_half(value):
    return pltpu.roll(value, H, value.ndim - 1)


def low_lanes(shape):
    return lax.broadcasted_iota(jnp.int32, shape, len(shape) - 1) < H


def pack_left(top, bottom, low):
    return jnp.where(low, top, bottom)


def pack_right(top, bottom, low):
    return jnp.where(low, bottom, top)


def pack_kernel(obj_ref, left_ref, right_ref):
    low = low_lanes((H, N))
    for i in range(2):
        for j in range(2):
            top = obj_ref[i, j, :H, :]
            bottom = swap_half(obj_ref[i, j, H:, :])
            left_ref[i, j] = pack_left(top, bottom, low)
            right_ref[i, j] = pack_right(top, bottom, low)


def rows_kernel(obj_ref, from_left_ref, from_right_ref, up_ref, down_ref):
    low = low_lanes((H, N))
    for i in range(2):
        for j in range(2):
            first, second = from_right_ref[i, j], from_left_ref[i, j]
            up_ref[i, j, :, :N] = obj_ref[i, j, :H, :]
            up_ref[i, j, :, N:] = jnp.where(low, first, second)
            down_ref[i, j, :, :N] = obj_ref[i, j, H:, :]
            down_ref[i, j, :, N:] = swap_half(jnp.where(low, second, first))


def split(value):
    high = value.astype(BF16)
    return high, (value - high.astype(F32)).astype(BF16)


def dot(a, b):
    return jnp.dot(a, b, preferred_element_type=F32)


def from_right(value, high, low):
    v_high, v_low = split(value)
    return dot(v_high, high) + (dot(v_low, high) + dot(v_high, low))


def from_left(high, low, value):
    v_high, v_low = split(value)
    return dot(high, v_high) + (dot(high, v_low) + dot(low, v_high))


def regroup(value):
    return jnp.concatenate(
        [
            jnp.concatenate([value[:N, :N], value[N:, :N]], axis=1),
            jnp.concatenate([value[:N, N:], value[N:, N:]], axis=1),
        ],
        axis=0,
    )


def main_kernel(
    scal_ref,
    up_ref,
    down_ref,
    above_ref,
    below_ref,
    probe_ref,
    kernel_ref,
    measured_ref,
    table_ref,
    mid_ref,
    high_ref,
    low_ref,
    ext,
    acc,
):
    for i in range(2):
        for j in range(2):
            k = 2 * i + j
            ext[k, 0:H, :] = above_ref[i, j]
            ext[k, H : 2 * H, :] = up_ref[i, j]
            ext[k, 2 * H : 3 * H, :] = down_ref[i, j]
            ext[k, 3 * H :, :] = below_ref[i, j]
    lane = lax.broadcasted_iota(jnp.int32, (N + 8, N), 1)
    live = scal_ref[4]
    sub = lax.broadcasted_iota(jnp.int32, (N // 8, 8, N), 1)
    rows, turns, masks = [], [], []
    for slot in range(2):
        row, column = scal_ref[2 * slot], scal_ref[2 * slot + 1]
        turn = jnp.where(column < H, column + H, column - H)
        masks.append((lane >= turn) != (column < H))
        rows.append(row)
        turns.append(turn)

    def align(slot):
        odd = lax.rem(rows[slot], 8)
        return pl.multiple_of(rows[slot] - odd, 8), odd

    def cut(k, slot):
        back = jnp.where(turns[slot] == 0, 0, N - turns[slot])
        start, odd = align(slot)
        first = pltpu.roll(ext[k, pl.ds(start, N + 8), :N], back, 1)
        second = pltpu.roll(ext[k, pl.ds(start, N + 8), N:], back, 1)
        inside = (lane < N - turns[slot]) != (scal_ref[2 * slot + 1] < H)
        value = jnp.where(inside, first, second).reshape(N // 8 + 1, 8, N)
        value = pltpu.roll(value, jnp.where(odd == 0, 0, 8 - odd), 1)
        return jnp.where(sub < 8 - odd, value[:-1], value[1:]).reshape(N, N)

    def both(j):
        re = jnp.concatenate([cut(j, 0), cut(j, 1)], axis=0)
        im = jnp.concatenate([cut(2 + j, 0), cut(2 + j, 1)], axis=0)
        return re, im

    def twice(value):
        return jnp.concatenate([value, value], axis=0)

    f_high, f_low, b_high, b_low = (table_ref[i] for i in range(4))

    def join(re, im):
        return jnp.concatenate([re, im], axis=1)

    def forward(re, im):
        half = from_right(join(re, im), f_high, f_low)
        out = from_left(b_high, b_low, regroup(half))
        return out[:N], out[N:]

    def backward(re, im):
        half = from_left(f_high, f_low, jnp.concatenate([re, im], axis=0))
        out = from_right(regroup(half), b_high, b_low)
        return out[:, :N], out[:, N:]

    probe_re, probe_im = twice(probe_ref[0]), twice(probe_ref[1])
    k_re = jnp.concatenate([kernel_ref[0], kernel_ref[0]], axis=1)
    k_im = jnp.concatenate([kernel_ref[1], kernel_ref[1]], axis=1)
    t_re, t_im = both(0)
    w_re = t_re * probe_re - t_im * probe_im
    w_im = t_re * probe_im + t_im * probe_re
    s_re, s_im = forward(w_re, w_im)
    s_re, s_im = k_re * s_re - k_im * s_im, k_re * s_im + k_im * s_re
    p_re, p_im = backward(s_re, s_im)
    t_re, t_im = both(1)
    w_re = t_re * p_re - t_im * p_im
    w_im = t_re * p_im + t_im * p_re
    far_re, far_im = forward(w_re, w_im)
    target = jnp.concatenate([measured_ref[0], measured_ref[1]], axis=1)
    misfit = far_re * far_re + far_im * far_im - target
    g_re, g_im = backward(misfit * far_re, misfit * far_im)

    def add(k, value):
        for slot in range(2):
            turned = pltpu.roll(value[slot * N : (slot + 1) * N], turns[slot], 1)
            turned = jnp.where(slot < live, turned, 0.0)
            start, odd = align(slot)
            turned = pltpu.roll(turned.reshape(N // 8, 8, N), odd, 1)
            none = jnp.zeros((1, 8, N), F32)
            turned = jnp.concatenate(
                [
                    jnp.where(sub[:1] < odd, none, turned[:1]),
                    jnp.where(sub[1:] < odd, turned[:-1], turned[1:]),
                    jnp.where(sub[:1] < odd, turned[-1:], none),
                ],
                axis=0,
            ).reshape(N + 8, N)
            where = pl.ds(start, N + 8)
            acc[k, where, :N] += jnp.where(masks[slot], turned, 0.0)
            acc[k, where, N:] += jnp.where(masks[slot], 0.0, turned)

    acc[...] = jnp.zeros_like(acc)
    add(1, p_re * g_re + p_im * g_im)
    add(3, p_re * g_im - p_im * g_re)
    g_re, g_im = t_re * g_re + t_im * g_im, t_re * g_im - t_im * g_re
    s_re, s_im = forward(g_re, g_im)
    s_re, s_im = k_re * s_re + k_im * s_im, k_re * s_im - k_im * s_re
    g_re, g_im = backward(s_re, s_im)
    add(0, probe_re * g_re + probe_im * g_im)
    add(2, probe_re * g_im - probe_im * g_re)
    for i in range(2):
        for j in range(2):
            k = 2 * i + j
            low_ref[i, j] = acc[k, 0:H, :]
            mid_ref[i, j] = acc[k, H : 3 * H, :]
            high_ref[i, j] = acc[k, 3 * H :, :]


def fold_rows_kernel(mid_ref, above_ref, below_ref, own_ref, left_ref, right_ref):
    low = low_lanes((H, N))
    for i in range(2):
        for j in range(2):
            top = mid_ref[i, j, :H, :] + above_ref[i, j]
            bottom = mid_ref[i, j, H:, :] + below_ref[i, j]
            own_ref[i, j, :H, :] = top[:, :N]
            own_ref[i, j, H:, :] = bottom[:, :N]
            top, bottom = top[:, N:], swap_half(bottom[:, N:])
            right_ref[i, j] = pack_left(top, bottom, low)
            left_ref[i, j] = pack_right(top, bottom, low)


def fold_columns_kernel(own_ref, from_left_ref, from_right_ref, out_ref):
    low = low_lanes((H, N))
    for i in range(2):
        for j in range(2):
            first, second = from_left_ref[i, j], from_right_ref[i, j]
            out_ref[i, j, :H, :] = own_ref[i, j, :H, :] + jnp.where(low, first, second)
            out_ref[i, j, H:, :] = own_ref[i, j, H:, :] + swap_half(
                jnp.where(low, second, first)
            )


def call(body, shapes, *operands, specs=None, scratch=(), name=None, flops=0):
    outs = [jax.ShapeDtypeStruct(shape, F32) for shape in shapes]
    size = 4 * sum(math.prod(s) for s in shapes) + sum(4 * o.size for o in operands)
    return pl.pallas_call(
        body,
        out_shape=outs,
        in_specs=specs or [VMEM] * len(operands),
        out_specs=[VMEM] * len(outs),
        scratch_shapes=list(scratch),
        compiler_params=pltpu.CompilerParams(vmem_limit_bytes=32 * 2**20),
        cost_estimate=pl.CostEstimate(flops=flops, bytes_accessed=size, transcendentals=0),
        name=name,
    )(*operands)


def to_next(value, axis):
    count = lax.axis_size(axis)
    return lax.ppermute(value, axis, [(i, i + 1) for i in range(count - 1)])


def to_previous(value, axis):
    count = lax.axis_size(axis)
    return lax.ppermute(value, axis, [(i + 1, i) for i in range(count - 1)])


def per_device(obj_slices, probe_wave, prop_phase, measured, positions, counts):
    packed = (2, 2, H, N)
    strip = (2, 2, H, 2 * N)
    tile = (2, 2, N, N)
    local_y = positions[0, 0, 0] - lax.axis_index("row") * N + H
    local_x = positions[0, 0, 1] - lax.axis_index("col") * N + H
    scalars = jnp.stack([local_y[0], local_x[0], local_y[1], local_x[1], counts[0, 0]])
    kernel = jnp.stack([jnp.cos(prop_phase), jnp.sin(prop_phase)])
    tables = jnp.asarray(dft_tables())

    left, right = call(pack_kernel, [packed] * 2, obj_slices, name="pack_columns")
    from_left, from_right = to_next(right, "col"), to_previous(left, "col")
    up, down = call(
        rows_kernel, [strip] * 2, obj_slices, from_left, from_right, name="pack_rows"
    )
    above, below = to_next(down, "row"), to_previous(up, "row")
    mid, high, low = call(
        main_kernel,
        [(2, 2, N, 2 * N), strip, strip],
        scalars,
        up,
        down,
        above,
        below,
        probe_wave,
        kernel,
        measured[0, 0],
        tables,
        specs=[SMEM] + [VMEM] * 8,
        scratch=[pltpu.VMEM((4, 2 * N, 2 * N), F32), pltpu.VMEM((4, 2 * N, 2 * N), F32)],
        name="window_gradients",
        flops=36 * 2 * 256**3,
    )
    above, below = to_next(high, "row"), to_previous(low, "row")
    own, left, right = call(
        fold_rows_kernel, [tile, packed, packed], mid, above, below, name="fold_rows"
    )
    from_left, from_right = to_next(right, "col"), to_previous(left, "col")
    (out,) = call(
        fold_columns_kernel, [tile], own, from_left, from_right, name="fold_columns"
    )
    return out


def solution(mesh):
    placed = (
        P(None, None, "row", "col"),
        P(),
        P(),
        P("row", "col", None, None, None),
        P("row", "col", None, None),
        P("row", "col"),
    )
    return jax.shard_map(
        per_device,
        mesh=mesh,
        in_specs=placed,
        out_specs=P(None, None, "row", "col"),
        check_vma=False,
    )
```

time: 126 us -> 66.5 us (0.53)
  the two profiles are of different devices: /device:TPU:15 before, /device:TPU:31 now
where the time goes in v1:
time: 66.5 us; the launch traced here: 66.1 us
  starting transfers between devices  42.4 us (64%)
  waiting for transfers between devices  11.9 us (18%)
  Pallas kernels  5.88 us (9%)
  local copies, waits for them, and re-layouts  4.38 us (7%)
  between operations  0.81 us (1%)
  other arithmetic  0.77 us (1%)
    ppermute x4, starting transfers between devices, to_previous(): return lax.ppermute(value, axis, [(i + 1, i) for i in range(count - 1)])  26.4 us
    ppermute x4, starting transfers between devices, to_next(): return lax.ppermute(value, axis, [(i, i + 1) for i in range(count - 1)])  16 us
    ppermute x4, waiting for transfers between devices, to_previous(): return lax.ppermute(value, axis, [(i + 1, i) for i in range(count - 1)])  8.93 us
    pallas_call x5, Pallas kernels, call(): pl.pallas_call(body, out_shape=outs, in_specs=specs or [VMEM] * len(opera...  5.88 us
    ppermute x4, waiting for transfers between devices, to_next(): return lax.ppermute(value, axis, [(i, i + 1) for i in range(count - 1)])  2.96 us
    another operation x1, local copies, waits for them, and re-layouts, per_device(): jnp.stack([local_y[0], local_x[0], local_y[1], local_x[1], counts[0, 0]])  2.54 us
  transfers between devices with their start and end apart: 8, of which 6 were waited for; matrix products, arithmetic and copies ran while one was open for 6% of the time, Pallas kernels for 0%

profile of v1, /device:TPU:31, one launch (start us, length us, event | category | flops | bytes accessed | tf_op | source)
XLA Modules:
  0.0 66.1 jit_solution(618742348320004289)
XLA Ops:
  0.0 0.9 %copy-done = f32[2,2,128,128]{3,2,1,0:T(8,128)S(1)} copy-done((f32[2,2,128,128]{3,2,1,0:T(8,128)S(1)}, f32[2,2,128,128]{3,2,1,0:T(8,128)}, u32[]{:S(2)}) %copy-start) | copy-done | bytes 262168
  1.0 0.1 pack_columns.1
  1.1 4.1 %collective-permute-start = (f32[2,2,64,128]{3,2,1,0:T(8,128)S(1)}, f32[2,2,64,128]{3,2,1,0:T(8,128)S(1)}, u32[]{:S(2)}, u32[]{:S(2)}) collective-permute-start(f32[2,2,64,128]{3,2,1,0:T(8,128)S(1)} %get-tuple-element.15), channel_id=1, source_target_pairs={{0,1},{1,2},{2,3},{3,4},{4,5},{5,6},{6,7},{7,8},{8,9},{9,10},{10,1... | collective-permute-start | bytes 393224 | tf_op jit(solution)/shard_map/ppermute | solution.py:262
  5.2 16.1 %collective-permute-start.1 = (f32[2,2,64,128]{3,2,1,0:T(8,128)S(1)}, f32[2,2,64,128]{3,2,1,0:T(8,128)S(1)}, u32[]{:S(2)}, u32[]{:S(2)}) collective-permute-start(f32[2,2,64,128]{3,2,1,0:T(8,128)S(1)} %get-tuple-element.16), channel_id=1, source_target_pairs={{1,0},{2,1},{3,2},{4,3},{5,4},{6,5},{7,6},{8,7},{9,8},{10,9},{11,1... | collective-permute-start | bytes 393224 | tf_op jit(solution)/shard_map/ppermute | solution.py:267
  21.4 0.8 %subtract_add_fusion = (s32[1,1,1,2]{3,2,1,0:T(1,128)S(1)}, s32[1,1,1,2]{3,2,1,0:T(1,128)S(1)}) fusion(s32[1,1,2,2]{3,2,1,0:T(2,128)} %param.11, s32[]{:T(128)S(6)} %mul.7, s32[]{:T(128)S(6)} %mul.6), kind=kLoop, calls=%fused_computation.3 | loop fusion | flops 8 | bytes 40 | tf_op jit(solution)/shard_map/add | solution.py:275
  22.8 0.6 fusion
  23.4 2.5 %stack.12.scal_ref = s32[5]{0:T(128)S(1)} concatenate(s32[1]{0:T(128)} %bitcast, s32[1]{0:T(128)} %bitcast.1, s32[1]{0:T(128)} %bitcast.2, s32[1]{0:T(128)} %bitcast.3, s32[1]{0:T(128)} %bitcast.10), dimensions={0} | concatenate | bytes 40 | tf_op jit(solution)/shard_map/stack | solution.py:276
  25.9 0.1 pack_rows.1
  26.1 2.9 %collective-permute-start.3 = (f32[2,2,64,256]{3,2,1,0:T(8,128)S(1)}, f32[2,2,64,256]{3,2,1,0:T(8,128)S(1)}, u32[]{:S(2)}, u32[]{:S(2)}) collective-permute-start(f32[2,2,64,256]{3,2,1,0:T(8,128)S(1)} %get-tuple-element.17.up_ref), channel_id=1, source_target_pairs={{64,0},{128,64},{192,128},{256,192},{320,256},{384,320},{448,384},... | collective-permute-start | bytes 786440 | tf_op jit(solution)/shard_map/ppermute | solution.py:267
  28.9 4.3 %collective-permute-start.2 = (f32[2,2,64,256]{3,2,1,0:T(8,128)S(1)}, f32[2,2,64,256]{3,2,1,0:T(8,128)S(1)}, u32[]{:S(2)}, u32[]{:S(2)}) collective-permute-start(f32[2,2,64,256]{3,2,1,0:T(8,128)S(1)} %get-tuple-element.18.down_ref), channel_id=1, source_target_pairs={{0,64},{64,128},{128,192},{192,256},{256,320},{320,384},{384,448},... | collective-permute-start | bytes 786440 | tf_op jit(solution)/shard_map/ppermute | solution.py:262
  33.3 0.2 cosine_bitcast_fusion
  33.5 1.8 %collective-permute-done.3.below_ref = f32[2,2,64,256]{3,2,1,0:T(8,128)S(1)} collective-permute-done((f32[2,2,64,256]{3,2,1,0:T(8,128)S(1)}, f32[2,2,64,256]{3,2,1,0:T(8,128)S(1)}, u32[]{:S(2)}, u32[]{:S(2)}) %collective-permute-start.3) | collective-permute-done | bytes 262176 | tf_op jit(solution)/shard_map/ppermute | solution.py:267
  35.4 1.2 %collective-permute-done.2.above_ref = f32[2,2,64,256]{3,2,1,0:T(8,128)S(1)} collective-permute-done((f32[2,2,64,256]{3,2,1,0:T(8,128)S(1)}, f32[2,2,64,256]{3,2,1,0:T(8,128)S(1)}, u32[]{:S(2)}, u32[]{:S(2)}) %collective-permute-start.2) | collective-permute-done | bytes 262176 | tf_op jit(solution)/shard_map/ppermute | solution.py:262
  36.6 4.8 %window_gradients.1 = (f32[2,2,128,256]{3,2,1,0:T(8,128)S(1)}, f32[2,2,64,256]{3,2,1,0:T(8,128)S(1)}, f32[2,2,64,256]{3,2,1,0:T(8,128)S(1)}) custom-call(s32[5]{0:T(128)S(1)} %stack.12.scal_ref, f32[2,2,64,256]{3,2,1,0:T(8,128)S(1)} %get-tuple-element.17.up_ref, f32[2,2,64,256]{3,2,1,0:T(8,128)S(1)} %get-tuple-element.18.down_ref, ...), custom_call_target="tpu_custom_call" | custom-call | flops 1207959552 | bytes 3538964 | tf_op jit(solution)/shard_map/window_gradients/pallas_call | solution.py:248
  41.3 5.6 %collective-permute-start.4 = (f32[2,2,64,256]{3,2,1,0:T(8,128)S(1)}, f32[2,2,64,256]{3,2,1,0:T(8,128)S(1)}, u32[]{:S(2)}, u32[]{:S(2)}) collective-permute-start(f32[2,2,64,256]{3,2,1,0:T(8,128)S(1)} %get-tuple-element.20), channel_id=1, source_target_pairs={{0,64},{64,128},{128,192},{192,256},{256,320},{320,384},{384,448},... | collective-permute-start | bytes 786440 | tf_op jit(solution)/shard_map/ppermute | solution.py:262
  46.9 1.9 %collective-permute-start.5 = (f32[2,2,64,256]{3,2,1,0:T(8,128)S(1)}, f32[2,2,64,256]{3,2,1,0:T(8,128)S(1)}, u32[]{:S(2)}, u32[]{:S(2)}) collective-permute-start(f32[2,2,64,256]{3,2,1,0:T(8,128)S(1)} %get-tuple-element.21), channel_id=1, source_target_pairs={{64,0},{128,64},{192,128},{256,192},{320,256},{384,320},{448,384},... | collective-permute-start | bytes 786440 | tf_op jit(solution)/shard_map/ppermute | solution.py:267
  48.9 1.4 %collective-permute-done.4.above_ref = f32[2,2,64,256]{3,2,1,0:T(8,128)S(1)} collective-permute-done((f32[2,2,64,256]{3,2,1,0:T(8,128)S(1)}, f32[2,2,64,256]{3,2,1,0:T(8,128)S(1)}, u32[]{:S(2)}, u32[]{:S(2)}) %collective-permute-start.4) | collective-permute-done | bytes 262176 | tf_op jit(solution)/shard_map/ppermute | solution.py:262
  50.2 5.6 %collective-permute-done.5.below_ref = f32[2,2,64,256]{3,2,1,0:T(8,128)S(1)} collective-permute-done((f32[2,2,64,256]{3,2,1,0:T(8,128)S(1)}, f32[2,2,64,256]{3,2,1,0:T(8,128)S(1)}, u32[]{:S(2)}, u32[]{:S(2)}) %collective-permute-start.5) | collective-permute-done | bytes 262176 | tf_op jit(solution)/shard_map/ppermute | solution.py:267
  55.8 0.1 fold_rows.1
  55.9 1.9 %collective-permute-start.6 = (f32[2,2,64,128]{3,2,1,0:T(8,128)S(1)}, f32[2,2,64,128]{3,2,1,0:T(8,128)S(1)}, u32[]{:S(2)}, u32[]{:S(2)}) collective-permute-start(f32[2,2,64,128]{3,2,1,0:T(8,128)S(1)} %get-tuple-element.23), channel_id=1, source_target_pairs={{0,1},{1,2},{2,3},{3,4},{4,5},{5,6},{6,7},{7,8},{8,9},{9,10},{10,1... | collective-permute-start | bytes 393224 | tf_op jit(solution)/shard_map/ppermute | solution.py:262
  57.9 5.5 %collective-permute-start.7 = (f32[2,2,64,128]{3,2,1,0:T(8,128)S(1)}, f32[2,2,64,128]{3,2,1,0:T(8,128)S(1)}, u32[]{:S(2)}, u32[]{:S(2)}) collective-permute-start(f32[2,2,64,128]{3,2,1,0:T(8,128)S(1)} %get-tuple-element.24), channel_id=1, source_target_pairs={{1,0},{2,1},{3,2},{4,3},{5,4},{6,5},{7,6},{8,7},{9,8},{10,9},{11,1... | collective-permute-start | bytes 393224 | tf_op jit(solution)/shard_map/ppermute | solution.py:267
  63.4 0.4 collective-permute-done.6.from_left_ref
  63.8 1.5 %collective-permute-done.7.from_right_ref = f32[2,2,64,128]{3,2,1,0:T(8,128)S(1)} collective-permute-done((f32[2,2,64,128]{3,2,1,0:T(8,128)S(1)}, f32[2,2,64,128]{3,2,1,0:T(8,128)S(1)}, u32[]{:S(2)}, u32[]{:S(2)}) %collective-permute-start.7) | collective-permute-done | bytes 131104 | tf_op jit(solution)/shard_map/ppermute | solution.py:267
  65.3 0.8 %fold_columns.1 = f32[2,2,128,128]{3,2,1,0:T(8,128)} custom-call(f32[2,2,128,128]{3,2,1,0:T(8,128)S(1)} %get-tuple-element.22.own_ref, f32[2,2,64,128]{3,2,1,0:T(8,128)S(1)} %collective-permute-done.6.from_left_ref, f32[2,2,64,128]{3,2,1,0:T(8,128)S(1)} %collective-permute-done.7.from_right_ref), custom_call_target="tpu_custom_call" | custom-call | bytes 786432 | tf_op jit(solution)/shard_map/fold_columns/pallas_call | solution.py:248
  (14 shorter events, 0.0 us)
Async XLA Ops:
  0.0 0.9 %copy-start = (f32[2,2,128,128]{3,2,1,0:T(8,128)S(1)}, f32[2,2,128,128]{3,2,1,0:T(8,128)}, u32[]{:S(2)}) copy-start(f32[2,2,128,128]{3,2,1,0:T(8,128)} %obj_ref.3) | copy-start | bytes 786436
  1.0 25.0 %copy-start.1 = (f32[2,2,128,128]{3,2,1,0:T(8,128)S(1)}, f32[2,2,128,128]{3,2,1,0:T(8,128)}, u32[]{:S(2)}) copy-start(f32[2,2,128,128]{3,2,1,0:T(8,128)} %obj_ref.3) | copy-start | bytes 786436
  1.0 32.3 %copy-start.5 = (f32[128,128]{1,0:T(8,128)S(1)}, f32[128,128]{1,0:T(8,128)}, u32[]{:S(2)}) copy-start(f32[128,128]{1,0:T(8,128)} %param.9) | copy-start | bytes 196612
  1.1 35.5 %copy-start.4 = (bf16[4,256,256]{2,1,0:T(8,128)(2,1)S(1)}, bf16[4,256,256]{2,1,0:T(8,128)(2,1)}, u32[]{:S(2)}) copy-start(bf16[4,256,256]{2,1,0:T(8,128)(2,1)} %constant.15.clone.table_ref) | copy-start | bytes 1572868
  1.1 24.9 %collective-permute-start = (f32[2,2,64,128]{3,2,1,0:T(8,128)S(1)}, f32[2,2,64,128]{3,2,1,0:T(8,128)S(1)}, u32[]{:S(2)}, u32[]{:S(2)}) collective-permute-start(f32[2,2,64,128]{3,2,1,0:T(8,128)S(1)} %get-tuple-element.15), channel_id=1, source_target_pairs={{0,1},{1,2},{2,3},{3,4},{4,5},{5,6},{6,7},{7,8},{8,9},{9,10},{10,1... | collective-permute-start | bytes 393224 | tf_op jit(solution)/shard_map/ppermute | solution.py:262
  5.2 20.7 %collective-permute-start.1 = (f32[2,2,64,128]{3,2,1,0:T(8,128)S(1)}, f32[2,2,64,128]{3,2,1,0:T(8,128)S(1)}, u32[]{:S(2)}, u32[]{:S(2)}) collective-permute-start(f32[2,2,64,128]{3,2,1,0:T(8,128)S(1)} %get-tuple-element.16), channel_id=1, source_target_pairs={{1,0},{2,1},{3,2},{4,3},{5,4},{6,5},{7,6},{8,7},{9,8},{10,9},{11,1... | collective-permute-start | bytes 393224 | tf_op jit(solution)/shard_map/ppermute | solution.py:267
  26.1 9.3 %collective-permute-start.3 = (f32[2,2,64,256]{3,2,1,0:T(8,128)S(1)}, f32[2,2,64,256]{3,2,1,0:T(8,128)S(1)}, u32[]{:S(2)}, u32[]{:S(2)}) collective-permute-start(f32[2,2,64,256]{3,2,1,0:T(8,128)S(1)} %get-tuple-element.17.up_ref), channel_id=1, source_target_pairs={{64,0},{128,64},{192,128},{256,192},{320,256},{384,320},{448,384},... | collective-permute-start | bytes 786440 | tf_op jit(solution)/shard_map/ppermute | solution.py:267
  28.9 7.6 %collective-permute-start.2 = (f32[2,2,64,256]{3,2,1,0:T(8,128)S(1)}, f32[2,2,64,256]{3,2,1,0:T(8,128)S(1)}, u32[]{:S(2)}, u32[]{:S(2)}) collective-permute-start(f32[2,2,64,256]{3,2,1,0:T(8,128)S(1)} %get-tuple-element.18.down_ref), channel_id=1, source_target_pairs={{0,64},{64,128},{128,192},{192,256},{256,320},{320,384},{384,448},... | collective-permute-start | bytes 786440 | tf_op jit(solution)/shard_map/ppermute | solution.py:262
  33.5 3.0 %copy-start.2 = (f32[2,128,128]{2,1,0:T(8,128)S(1)}, f32[2,128,128]{2,1,0:T(8,128)}, u32[]{:S(2)}) copy-start(f32[2,128,128]{2,1,0:T(8,128)} %probe_ref.1) | copy-start | bytes 393220
  33.5 3.0 %copy-start.3 = (f32[1,1,2,128,128]{4,3,2,1,0:T(8,128)S(1)}, f32[1,1,2,128,128]{4,3,2,1,0:T(8,128)}, u32[]{:S(2)}) copy-start(f32[1,1,2,128,128]{4,3,2,1,0:T(8,128)} %param.10) | copy-start | bytes 393220
  41.3 8.9 %collective-permute-start.4 = (f32[2,2,64,256]{3,2,1,0:T(8,128)S(1)}, f32[2,2,64,256]{3,2,1,0:T(8,128)S(1)}, u32[]{:S(2)}, u32[]{:S(2)}) collective-permute-start(f32[2,2,64,256]{3,2,1,0:T(8,128)S(1)} %get-tuple-element.20), channel_id=1, source_target_pairs={{0,64},{64,128},{128,192},{192,256},{256,320},{320,384},{384,448},... | collective-permute-start | bytes 786440 | tf_op jit(solution)/shard_map/ppermute | solution.py:262
  46.9 8.9 %collective-permute-start.5 = (f32[2,2,64,256]{3,2,1,0:T(8,128)S(1)}, f32[2,2,64,256]{3,2,1,0:T(8,128)S(1)}, u32[]{:S(2)}, u32[]{:S(2)}) collective-permute-start(f32[2,2,64,256]{3,2,1,0:T(8,128)S(1)} %get-tuple-element.21), channel_id=1, source_target_pairs={{64,0},{128,64},{192,128},{256,192},{320,256},{384,320},{448,384},... | collective-permute-start | bytes 786440 | tf_op jit(solution)/shard_map/ppermute | solution.py:267
  55.9 7.8 %collective-permute-start.6 = (f32[2,2,64,128]{3,2,1,0:T(8,128)S(1)}, f32[2,2,64,128]{3,2,1,0:T(8,128)S(1)}, u32[]{:S(2)}, u32[]{:S(2)}) collective-permute-start(f32[2,2,64,128]{3,2,1,0:T(8,128)S(1)} %get-tuple-element.23), channel_id=1, source_target_pairs={{0,1},{1,2},{2,3},{3,4},{4,5},{5,6},{6,7},{7,8},{8,9},{9,10},{10,1... | collective-permute-start | bytes 393224 | tf_op jit(solution)/shard_map/ppermute | solution.py:262
  57.9 7.4 %collective-permute-start.7 = (f32[2,2,64,128]{3,2,1,0:T(8,128)S(1)}, f32[2,2,64,128]{3,2,1,0:T(8,128)S(1)}, u32[]{:S(2)}, u32[]{:S(2)}) collective-permute-start(f32[2,2,64,128]{3,2,1,0:T(8,128)S(1)} %get-tuple-element.24), channel_id=1, source_target_pairs={{1,0},{2,1},{3,2},{4,3},{5,4},{6,5},{7,6},{8,7},{9,8},{10,9},{11,1... | collective-permute-start | bytes 393224 | tf_op jit(solution)/shard_map/ppermute | solution.py:267

commit v2 on v1

--- a/solution.py
+++ b/solution.py
@@ -36,33 +36,40 @@
     return lax.broadcasted_iota(jnp.int32, shape, len(shape) - 1) < H
 
 
-def pack_left(top, bottom, low):
-    return jnp.where(low, top, bottom)
-
-
-def pack_right(top, bottom, low):
-    return jnp.where(low, bottom, top)
-
-
-def pack_kernel(obj_ref, left_ref, right_ref):
-    low = low_lanes((H, N))
-    for i in range(2):
-        for j in range(2):
-            top = obj_ref[i, j, :H, :]
-            bottom = swap_half(obj_ref[i, j, H:, :])
-            left_ref[i, j] = pack_left(top, bottom, low)
-            right_ref[i, j] = pack_right(top, bottom, low)
-
-
-def rows_kernel(obj_ref, from_left_ref, from_right_ref, up_ref, down_ref):
-    low = low_lanes((H, N))
-    for i in range(2):
-        for j in range(2):
-            first, second = from_right_ref[i, j], from_left_ref[i, j]
-            up_ref[i, j, :, :N] = obj_ref[i, j, :H, :]
-            up_ref[i, j, :, N:] = jnp.where(low, first, second)
-            down_ref[i, j, :, :N] = obj_ref[i, j, H:, :]
-            down_ref[i, j, :, N:] = swap_half(jnp.where(low, second, first))
+def parity_of(axis):
+    return lax.rem(lax.axis_index(axis), 2)
+
+
+def pack_columns(top, bottom, parity):
+    bottom = swap_half(bottom)
+    low = low_lanes((H, N)) != (parity == 1)
+    return jnp.where(low, bottom, top), jnp.where(low, top, bottom)
+
+
+def unpack_columns(even, odd, parity):
+    low = low_lanes((H, N)) != (parity == 1)
+    return jnp.where(low, even, odd), swap_half(jnp.where(low, odd, even))
+
+
+def pack_kernel(obj_ref, even_ref, odd_ref):
+    parity = parity_of("col")
+    for i in range(2):
+        for j in range(2):
+            even_ref[i, j], odd_ref[i, j] = pack_columns(
+                obj_ref[i, j, :H, :], obj_ref[i, j, H:, :], parity
+            )
+
+
+def rows_kernel(obj_ref, even_ref, odd_ref, row_even_ref, row_odd_ref):
+    parity = parity_of("col")
+    row_parity = parity_of("row")
+    for i in range(2):
+        for j in range(2):
+            top, bottom = unpack_columns(even_ref[1 - parity, i, j], odd_ref[i, j], parity)
+            top = jnp.concatenate([obj_ref[i, j, :H, :], top], axis=1)
+            bottom = jnp.concatenate([obj_ref[i, j, H:, :], bottom], axis=1)
+            row_even_ref[i, j] = jnp.where(row_parity == 0, bottom, top)
+            row_odd_ref[i, j] = jnp.where(row_parity == 0, top, bottom)
 
 
 def split(value):
@@ -95,37 +102,45 @@
 
 
 def main_kernel(
-    scal_ref,
-    up_ref,
-    down_ref,
-    above_ref,
-    below_ref,
+    positions_ref,
+    counts_ref,
+    own_even_ref,
+    own_odd_ref,
+    even_ref,
+    odd_ref,
     probe_ref,
     kernel_ref,
     measured_ref,
     table_ref,
     mid_ref,
-    high_ref,
-    low_ref,
+    to_even_ref,
+    to_odd_ref,
     ext,
     acc,
 ):
+    row_parity = parity_of("row")
+
+    def strip(number):
+        return pl.ds(pl.multiple_of(jnp.where(row_parity == 0, number, 3 - number) * H, H), H)
+
     for i in range(2):
         for j in range(2):
             k = 2 * i + j
-            ext[k, 0:H, :] = above_ref[i, j]
-            ext[k, H : 2 * H, :] = up_ref[i, j]
-            ext[k, 2 * H : 3 * H, :] = down_ref[i, j]
-            ext[k, 3 * H :, :] = below_ref[i, j]
+            ext[k, strip(0), :] = odd_ref[i, j]
+            ext[k, strip(1), :] = own_odd_ref[i, j]
+            ext[k, strip(2), :] = own_even_ref[i, j]
+            ext[k, strip(3), :] = even_ref[1 - row_parity, i, j]
     lane = lax.broadcasted_iota(jnp.int32, (N + 8, N), 1)
-    live = scal_ref[4]
+    live = counts_ref[0, 0]
     sub = lax.broadcasted_iota(jnp.int32, (N // 8, 8, N), 1)
-    rows, turns, masks = [], [], []
+    rows, turns, masks, wraps = [], [], [], []
     for slot in range(2):
-        row, column = scal_ref[2 * slot], scal_ref[2 * slot + 1]
+        row = positions_ref[0, 0, 0, slot] - lax.axis_index("row") * N + H
+        column = positions_ref[0, 0, 1, slot] - lax.axis_index("col") * N + H
         turn = jnp.where(column < H, column + H, column - H)
         masks.append((lane >= turn) != (column < H))
         rows.append(row)
+        wraps.append(column < H)
         turns.append(turn)
 
     def align(slot):
@@ -137,7 +152,7 @@
         start, odd = align(slot)
         first = pltpu.roll(ext[k, pl.ds(start, N + 8), :N], back, 1)
         second = pltpu.roll(ext[k, pl.ds(start, N + 8), N:], back, 1)
-        inside = (lane < N - turns[slot]) != (scal_ref[2 * slot + 1] < H)
+        inside = (lane < N - turns[slot]) != wraps[slot]
         value = jnp.where(inside, first, second).reshape(N // 8 + 1, 8, N)
         value = pltpu.roll(value, jnp.where(odd == 0, 0, 8 - odd), 1)
         return jnp.where(sub < 8 - odd, value[:-1], value[1:]).reshape(N, N)
@@ -213,33 +228,31 @@
     for i in range(2):
         for j in range(2):
             k = 2 * i + j
-            low_ref[i, j] = acc[k, 0:H, :]
             mid_ref[i, j] = acc[k, H : 3 * H, :]
-            high_ref[i, j] = acc[k, 3 * H :, :]
-
-
-def fold_rows_kernel(mid_ref, above_ref, below_ref, own_ref, left_ref, right_ref):
-    low = low_lanes((H, N))
-    for i in range(2):
-        for j in range(2):
-            top = mid_ref[i, j, :H, :] + above_ref[i, j]
-            bottom = mid_ref[i, j, H:, :] + below_ref[i, j]
+            to_even_ref[i, j] = acc[k, strip(3), :]
+            to_odd_ref[i, j] = acc[k, strip(0), :]
+
+
+def fold_rows_kernel(mid_ref, row_even_ref, row_odd_ref, own_ref, even_ref, odd_ref):
+    parity = parity_of("col")
+    row_parity = parity_of("row")
+    for i in range(2):
+        for j in range(2):
+            even, odd = row_even_ref[1 - row_parity, i, j], row_odd_ref[i, j]
+            top = mid_ref[i, j, :H, :] + jnp.where(row_parity == 0, odd, even)
+            bottom = mid_ref[i, j, H:, :] + jnp.where(row_parity == 0, even, odd)
             own_ref[i, j, :H, :] = top[:, :N]
             own_ref[i, j, H:, :] = bottom[:, :N]
-            top, bottom = top[:, N:], swap_half(bottom[:, N:])
-            right_ref[i, j] = pack_left(top, bottom, low)
-            left_ref[i, j] = pack_right(top, bottom, low)
-
-
-def fold_columns_kernel(own_ref, from_left_ref, from_right_ref, out_ref):
-    low = low_lanes((H, N))
-    for i in range(2):
-        for j in range(2):
-            first, second = from_left_ref[i, j], from_right_ref[i, j]
-            out_ref[i, j, :H, :] = own_ref[i, j, :H, :] + jnp.where(low, first, second)
-            out_ref[i, j, H:, :] = own_ref[i, j, H:, :] + swap_half(
-                jnp.where(low, second, first)
-            )
+            odd_ref[i, j], even_ref[i, j] = pack_columns(top[:, N:], bottom[:, N:], parity)
+
+
+def fold_columns_kernel(own_ref, even_ref, odd_ref, out_ref):
+    parity = parity_of("col")
+    for i in range(2):
+        for j in range(2):
+            top, bottom = unpack_columns(odd_ref[i, j], even_ref[1 - parity, i, j], parity)
+            out_ref[i, j, :H, :] = own_ref[i, j, :H, :] + top
+            out_ref[i, j, H:, :] = own_ref[i, j, H:, :] + bottom
 
 
 def call(body, shapes, *operands, specs=None, scratch=(), name=None, flops=0):
@@ -257,57 +270,48 @@
     )(*operands)
 
 
-def to_next(value, axis):
+def exchange(even, odd, axis):
     count = lax.axis_size(axis)
-    return lax.ppermute(value, axis, [(i, i + 1) for i in range(count - 1)])
-
-
-def to_previous(value, axis):
-    count = lax.axis_size(axis)
-    return lax.ppermute(value, axis, [(i + 1, i) for i in range(count - 1)])
+    pairs = [(i, i + 1) for i in range(1, count - 1, 2)]
+    odd = lax.ppermute(odd, axis, pairs + [(b, a) for a, b in pairs])
+    groups = [[i, i + 1] for i in range(0, count, 2)]
+    even = lax.all_gather(even, axis, axis_index_groups=groups)
+    return even, odd
 
 
 def per_device(obj_slices, probe_wave, prop_phase, measured, positions, counts):
     packed = (2, 2, H, N)
     strip = (2, 2, H, 2 * N)
     tile = (2, 2, N, N)
-    local_y = positions[0, 0, 0] - lax.axis_index("row") * N + H
-    local_x = positions[0, 0, 1] - lax.axis_index("col") * N + H
-    scalars = jnp.stack([local_y[0], local_x[0], local_y[1], local_x[1], counts[0, 0]])
     kernel = jnp.stack([jnp.cos(prop_phase), jnp.sin(prop_phase)])
     tables = jnp.asarray(dft_tables())
 
-    left, right = call(pack_kernel, [packed] * 2, obj_slices, name="pack_columns")
-    from_left, from_right = to_next(right, "col"), to_previous(left, "col")
-    up, down = call(
-        rows_kernel, [strip] * 2, obj_slices, from_left, from_right, name="pack_rows"
-    )
-    above, below = to_next(down, "row"), to_previous(up, "row")
-    mid, high, low = call(
+    strips = call(pack_kernel, [packed] * 2, obj_slices, name="pack_columns")
+    strips = exchange(*strips, "col")
+    own = call(rows_kernel, [strip] * 2, obj_slices, *strips, name="pack_rows")
+    strips = exchange(*own, "row")
+    mid, *strips = call(
         main_kernel,
         [(2, 2, N, 2 * N), strip, strip],
-        scalars,
-        up,
-        down,
-        above,
-        below,
+        positions,
+        counts,
+        *own,
+        *strips,
         probe_wave,
         kernel,
         measured[0, 0],
         tables,
-        specs=[SMEM] + [VMEM] * 8,
+        specs=[SMEM] * 2 + [VMEM] * 8,
         scratch=[pltpu.VMEM((4, 2 * N, 2 * N), F32), pltpu.VMEM((4, 2 * N, 2 * N), F32)],
         name="window_gradients",
         flops=36 * 2 * 256**3,
     )
-    above, below = to_next(high, "row"), to_previous(low, "row")
-    own, left, right = call(
-        fold_rows_kernel, [tile, packed, packed], mid, above, below, name="fold_rows"
-    )
-    from_left, from_right = to_next(right, "col"), to_previous(left, "col")
-    (out,) = call(
-        fold_columns_kernel, [tile], own, from_left, from_right, name="fold_columns"
-    )
+    strips = exchange(*strips, "row")
+    own, *strips = call(
+        fold_rows_kernel, [tile, packed, packed], mid, *strips, name="fold_rows"
+    )
+    strips = exchange(*strips, "col")
+    (out,) = call(fold_columns_kernel, [tile], own, *strips, name="fold_columns")
     return out
 
 

time: 66.5 us -> 59.1 us (0.89)
  the two profiles are of different devices: /device:TPU:31 before, /device:TPU:38 now
where the time goes in v2:
time: 59.1 us; the launch traced here: 58.8 us
  starting transfers between devices  25.9 us (44%)
  blocking collectives  16.2 us (27%)
  waiting for transfers between devices  8.09 us (14%)
  Pallas kernels  5.91 us (10%)
  local copies, waits for them, and re-layouts  1.88 us (3%)
  between operations  0.77 us (1%)
    ppermute x4, starting transfers between devices, exchange(): odd = lax.ppermute(odd, axis, pairs + [(b, a) for a, b in pairs])  25.9 us
    all_gather x4, blocking collectives, exchange(): even = lax.all_gather(even, axis, axis_index_groups=groups)  16.2 us
    ppermute x4, waiting for transfers between devices, exchange(): odd = lax.ppermute(odd, axis, pairs + [(b, a) for a, b in pairs])  8.09 us
    pallas_call x5, Pallas kernels, call(): pl.pallas_call(body, out_shape=outs, in_specs=specs or [VMEM] * len(opera...  5.91 us
    unnamed x12, local copies, waits for them, and re-layouts  1.64 us
  transfers between devices with their start and end apart: 4, of which 2 were waited for; matrix products, arithmetic and copies ran while one was open for 0% of the time, Pallas kernels for 0%

profile of v2, /device:TPU:38, one launch (start us, length us, event | category | flops | bytes accessed | tf_op | source)
XLA Modules:
  0.0 58.8 jit_solution(9257066006266959950)
XLA Ops:
  0.0 0.9 %copy-done = f32[2,2,128,128]{3,2,1,0:T(8,128)S(1)} copy-done((f32[2,2,128,128]{3,2,1,0:T(8,128)S(1)}, f32[2,2,128,128]{3,2,1,0:T(8,128)}, u32[]{:S(2)}) %copy-start) | copy-done | bytes 262168
  1.0 0.1 pack_columns.1
  1.1 18.5 %collective-permute-start = (f32[2,2,64,128]{3,2,1,0:T(8,128)S(1)}, f32[2,2,64,128]{3,2,1,0:T(8,128)S(1)}, u32[]{:S(2)}, u32[]{:S(2)}) collective-permute-start(f32[2,2,64,128]{3,2,1,0:T(8,128)S(1)} %get-tuple-element.16), channel_id=1, source_target_pairs={{1,2},{3,4},{5,6},{7,8},{9,10},{11,12},{13,14},{15,16},{17,18},{19... | collective-permute-start | bytes 393224 | tf_op jit(solution)/shard_map/ppermute | solution.py:276
  19.6 5.6 %all-gather = f32[4,2,64,128]{3,2,1,0:T(8,128)S(1)} all-gather(f32[2,2,64,128]{3,2,1,0:T(8,128)S(1)} %get-tuple-element.15), channel_id=2, replica_groups={{0,1},{2,3},{4,5},{6,7},{8,9},{10,11},{12,13},{14,15},{16,17},{18,19},{..., dimensions={0}, use_global_device_ids=true | all-gather | bytes 393216 | tf_op jit(solution)/shard_map/all_gather | solution.py:278
  25.2 0.0 collective-permute-done.odd_ref
  25.2 0.1 pack_rows.1
  25.3 1.9 %collective-permute-start.1 = (f32[2,2,64,256]{3,2,1,0:T(8,128)S(1)}, f32[2,2,64,256]{3,2,1,0:T(8,128)S(1)}, u32[]{:S(2)}, u32[]{:S(2)}) collective-permute-start(f32[2,2,64,256]{3,2,1,0:T(8,128)S(1)} %get-tuple-element.18.own_odd_ref), channel_id=1, source_target_pairs={{64,128},{192,256},{320,384},{448,512},{576,640},{704,768},{832,89... | collective-permute-start | bytes 786440 | tf_op jit(solution)/shard_map/ppermute | solution.py:276
  27.2 0.0 copy-done.5
  27.3 0.2 cosine_bitcast_fusion
  28.2 0.0 copy-start.4
  28.2 0.0 copy-start.1
  28.2 0.0 copy-start.2
  28.2 2.7 %all-gather.1 = f32[4,2,64,256]{3,2,1,0:T(8,128)S(1)} all-gather(f32[2,2,64,256]{3,2,1,0:T(8,128)S(1)} %get-tuple-element.17.own_even_ref), channel_id=3, replica_groups={{0,64},{128,192},{256,320},{384,448},{512,576},{640,704},{768,832},{896..., dimensions={0}, use_global_device_ids=true | all-gather | bytes 786432 | tf_op jit(solution)/shard_map/all_gather | solution.py:278
  30.9 3.3 %collective-permute-done.1.odd_ref = f32[2,2,64,256]{3,2,1,0:T(8,128)S(1)} collective-permute-done((f32[2,2,64,256]{3,2,1,0:T(8,128)S(1)}, f32[2,2,64,256]{3,2,1,0:T(8,128)S(1)}, u32[]{:S(2)}, u32[]{:S(2)}) %collective-permute-start.1) | collective-permute-done | bytes 262176 | tf_op jit(solution)/shard_map/ppermute | solution.py:276
  34.2 0.7 %copy-done.3 = s32[1,1,2,2]{3,2,1,0:T(2,128)S(1)} copy-done((s32[1,1,2,2]{3,2,1,0:T(2,128)S(1)}, s32[1,1,2,2]{3,2,1,0:T(2,128)}, u32[]{:S(2)}) %copy-start.3) | copy-done | bytes 40
  34.9 4.8 %window_gradients.1 = (f32[2,2,128,256]{3,2,1,0:T(8,128)S(1)}, f32[2,2,64,256]{3,2,1,0:T(8,128)S(1)}, f32[2,2,64,256]{3,2,1,0:T(8,128)S(1)}) custom-call(s32[1,1,2,2]{3,2,1,0:T(2,128)S(1)} %copy-done.3, s32[1,1]{1,0:T(1,128)S(6)} %copy.8.counts_ref, f32[2,2,64,256]{3,2,1,0:T(8,128)S(1)} %get-tuple-element.17.own_even_ref, ...), custom_call_target="tpu_custom_call" | custom-call | flops 1207959552 | bytes 3801108 | tf_op jit(solution)/shard_map/window_gradients/pallas_call | solution.py:261
  39.7 1.9 %collective-permute-start.2 = (f32[2,2,64,256]{3,2,1,0:T(8,128)S(1)}, f32[2,2,64,256]{3,2,1,0:T(8,128)S(1)}, u32[]{:S(2)}, u32[]{:S(2)}) collective-permute-start(f32[2,2,64,256]{3,2,1,0:T(8,128)S(1)} %get-tuple-element.21), channel_id=1, source_target_pairs={{64,128},{192,256},{320,384},{448,512},{576,640},{704,768},{832,89... | collective-permute-start | bytes 786440 | tf_op jit(solution)/shard_map/ppermute | solution.py:276
  41.6 2.2 %all-gather.2 = f32[4,2,64,256]{3,2,1,0:T(8,128)S(1)} all-gather(f32[2,2,64,256]{3,2,1,0:T(8,128)S(1)} %get-tuple-element.20), channel_id=4, replica_groups={{0,64},{128,192},{256,320},{384,448},{512,576},{640,704},{768,832},{896..., dimensions={0}, use_global_device_ids=true | all-gather | bytes 786432 | tf_op jit(solution)/shard_map/all_gather | solution.py:278
  43.8 4.8 %collective-permute-done.2.row_odd_ref = f32[2,2,64,256]{3,2,1,0:T(8,128)S(1)} collective-permute-done((f32[2,2,64,256]{3,2,1,0:T(8,128)S(1)}, f32[2,2,64,256]{3,2,1,0:T(8,128)S(1)}, u32[]{:S(2)}, u32[]{:S(2)}) %collective-permute-start.2) | collective-permute-done | bytes 262176 | tf_op jit(solution)/shard_map/ppermute | solution.py:276
  48.6 0.1 fold_rows.1
  48.7 3.6 %collective-permute-start.3 = (f32[2,2,64,128]{3,2,1,0:T(8,128)S(1)}, f32[2,2,64,128]{3,2,1,0:T(8,128)S(1)}, u32[]{:S(2)}, u32[]{:S(2)}) collective-permute-start(f32[2,2,64,128]{3,2,1,0:T(8,128)S(1)} %get-tuple-element.24), channel_id=1, source_target_pairs={{1,2},{3,4},{5,6},{7,8},{9,10},{11,12},{13,14},{15,16},{17,18},{19... | collective-permute-start | bytes 393224 | tf_op jit(solution)/shard_map/ppermute | solution.py:276
  52.3 5.6 %all-gather.3 = f32[4,2,64,128]{3,2,1,0:T(8,128)S(1)} all-gather(f32[2,2,64,128]{3,2,1,0:T(8,128)S(1)} %get-tuple-element.23), channel_id=5, replica_groups={{0,1},{2,3},{4,5},{6,7},{8,9},{10,11},{12,13},{14,15},{16,17},{18,19},{..., dimensions={0}, use_global_device_ids=true | all-gather | bytes 393216 | tf_op jit(solution)/shard_map/all_gather | solution.py:278
  57.9 0.0 collective-permute-done.3.odd_ref
  57.9 0.8 %fold_columns.1 = f32[2,2,128,128]{3,2,1,0:T(8,128)} custom-call(f32[2,2,128,128]{3,2,1,0:T(8,128)S(1)} %get-tuple-element.22.own_ref, f32[2,2,2,64,128]{4,3,2,1,0:T(8,128)S(1)} %bitcast.10, f32[2,2,64,128]{3,2,1,0:T(8,128)S(1)} %collective-permute-done.3.odd_ref), custom_call_target="tpu_custom_call" | custom-call | bytes 917504 | tf_op jit(solution)/shard_map/fold_columns/pallas_call | solution.py:261
  (7 shorter events, 0.0 us)
Async XLA Ops:
  0.0 0.9 %copy-start = (f32[2,2,128,128]{3,2,1,0:T(8,128)S(1)}, f32[2,2,128,128]{3,2,1,0:T(8,128)}, u32[]{:S(2)}) copy-start(f32[2,2,128,128]{3,2,1,0:T(8,128)} %obj_ref.3) | copy-start | bytes 786436
  1.1 24.1 %collective-permute-start = (f32[2,2,64,128]{3,2,1,0:T(8,128)S(1)}, f32[2,2,64,128]{3,2,1,0:T(8,128)S(1)}, u32[]{:S(2)}, u32[]{:S(2)}) collective-permute-start(f32[2,2,64,128]{3,2,1,0:T(8,128)S(1)} %get-tuple-element.16), channel_id=1, source_target_pairs={{1,2},{3,4},{5,6},{7,8},{9,10},{11,12},{13,14},{15,16},{17,18},{19... | collective-permute-start | bytes 393224 | tf_op jit(solution)/shard_map/ppermute | solution.py:276
  25.2 2.0 %copy-start.5 = (f32[128,128]{1,0:T(8,128)S(1)}, f32[128,128]{1,0:T(8,128)}, u32[]{:S(2)}) copy-start(f32[128,128]{1,0:T(8,128)} %param.9) | copy-start | bytes 196612
  25.3 8.9 %collective-permute-start.1 = (f32[2,2,64,256]{3,2,1,0:T(8,128)S(1)}, f32[2,2,64,256]{3,2,1,0:T(8,128)S(1)}, u32[]{:S(2)}, u32[]{:S(2)}) collective-permute-start(f32[2,2,64,256]{3,2,1,0:T(8,128)S(1)} %get-tuple-element.18.own_odd_ref), channel_id=1, source_target_pairs={{64,128},{192,256},{320,384},{448,512},{576,640},{704,768},{832,89... | collective-permute-start | bytes 786440 | tf_op jit(solution)/shard_map/ppermute | solution.py:276
  28.2 6.1 %copy-start.4 = (bf16[4,256,256]{2,1,0:T(8,128)(2,1)S(1)}, bf16[4,256,256]{2,1,0:T(8,128)(2,1)}, u32[]{:S(2)}) copy-start(bf16[4,256,256]{2,1,0:T(8,128)(2,1)} %constant.2.clone.table_ref) | copy-start | bytes 1572868
  28.2 6.0 %copy-start.1 = (f32[2,128,128]{2,1,0:T(8,128)S(1)}, f32[2,128,128]{2,1,0:T(8,128)}, u32[]{:S(2)}) copy-start(f32[2,128,128]{2,1,0:T(8,128)} %probe_ref.1) | copy-start | bytes 393220
  28.2 6.0 %copy-start.2 = (f32[1,1,2,128,128]{4,3,2,1,0:T(8,128)S(1)}, f32[1,1,2,128,128]{4,3,2,1,0:T(8,128)}, u32[]{:S(2)}) copy-start(f32[1,1,2,128,128]{4,3,2,1,0:T(8,128)} %param.10) | copy-start | bytes 393220
  34.2 0.7 %copy-start.3 = (s32[1,1,2,2]{3,2,1,0:T(2,128)S(1)}, s32[1,1,2,2]{3,2,1,0:T(2,128)}, u32[]{:S(2)}) copy-start(s32[1,1,2,2]{3,2,1,0:T(2,128)} %positions_ref.1) | copy-start | bytes 52
  39.7 8.9 %collective-permute-start.2 = (f32[2,2,64,256]{3,2,1,0:T(8,128)S(1)}, f32[2,2,64,256]{3,2,1,0:T(8,128)S(1)}, u32[]{:S(2)}, u32[]{:S(2)}) collective-permute-start(f32[2,2,64,256]{3,2,1,0:T(8,128)S(1)} %get-tuple-element.21), channel_id=1, source_target_pairs={{64,128},{192,256},{320,384},{448,512},{576,640},{704,768},{832,89... | collective-permute-start | bytes 786440 | tf_op jit(solution)/shard_map/ppermute | solution.py:276
  48.7 9.2 %collective-permute-start.3 = (f32[2,2,64,128]{3,2,1,0:T(8,128)S(1)}, f32[2,2,64,128]{3,2,1,0:T(8,128)S(1)}, u32[]{:S(2)}, u32[]{:S(2)}) collective-permute-start(f32[2,2,64,128]{3,2,1,0:T(8,128)S(1)} %get-tuple-element.24), channel_id=1, source_target_pairs={{1,2},{3,4},{5,6},{7,8},{9,10},{11,12},{13,14},{15,16},{17,18},{19... | collective-permute-start | bytes 393224 | tf_op jit(solution)/shard_map/ppermute | solution.py:276

commit v3 on v2

--- a/solution.py
+++ b/solution.py
@@ -13,7 +13,6 @@
 F32 = jnp.float32
 BF16 = jnp.bfloat16
 VMEM = pl.BlockSpec(memory_space=pltpu.VMEM)
-SMEM = pl.BlockSpec(memory_space=pltpu.SMEM)
 
 
 def dft_tables():
@@ -83,12 +82,20 @@
 
 def from_right(value, high, low):
     v_high, v_low = split(value)
-    return dot(v_high, high) + (dot(v_low, high) + dot(v_high, low))
+    out = []
+    for slot in (slice(0, N), slice(N, 2 * N)):
+        both = dot(jnp.concatenate([v_high[slot], v_low[slot]], axis=0), high)
+        out.append(both[:N] + (both[N:] + dot(v_high[slot], low)))
+    return jnp.concatenate(out, axis=0)
 
 
 def from_left(high, low, value):
     v_high, v_low = split(value)
-    return dot(high, v_high) + (dot(high, v_low) + dot(low, v_high))
+    out = []
+    for slot in (slice(0, N), slice(N, 2 * N)):
+        both = dot(high, jnp.concatenate([v_high[:, slot], v_low[:, slot]], axis=1))
+        out.append(both[:, :N] + (both[:, N:] + dot(low, v_high[:, slot])))
+    return jnp.concatenate(out, axis=1)
 
 
 def regroup(value):
@@ -101,15 +108,31 @@
     )
 
 
+def strip_rows(number):
+    number = jnp.where(parity_of("row") == 0, number, 3 - number)
+    return pl.ds(pl.multiple_of(number * H, H), H)
+
+
+def prepare_kernel(phase_ref, positions_ref, counts_ref, kernel_re_ref, kernel_im_ref, scal_ref):
+    kernel_re_ref[...] = jnp.cos(phase_ref[...])
+    kernel_im_ref[...] = jnp.sin(phase_ref[...])
+    for k, axis in enumerate(("row", "col")):
+        first = lax.axis_index(axis) * N - H
+        for slot in range(2):
+            value = positions_ref[0, 0, k : k + 1, slot : slot + 1] - first
+            scal_ref[2 * k + slot : 2 * k + slot + 1, :] = jnp.broadcast_to(value, (1, N))
+    scal_ref[4:5, :] = jnp.broadcast_to(counts_ref[...], (1, N))
+
+
 def main_kernel(
-    positions_ref,
-    counts_ref,
+    scal_ref,
     own_even_ref,
     own_odd_ref,
     even_ref,
     odd_ref,
     probe_ref,
-    kernel_ref,
+    kernel_re_ref,
+    kernel_im_ref,
     measured_ref,
     table_ref,
     mid_ref,
@@ -119,24 +142,20 @@
     acc,
 ):
     row_parity = parity_of("row")
-
-    def strip(number):
-        return pl.ds(pl.multiple_of(jnp.where(row_parity == 0, number, 3 - number) * H, H), H)
-
     for i in range(2):
         for j in range(2):
             k = 2 * i + j
-            ext[k, strip(0), :] = odd_ref[i, j]
-            ext[k, strip(1), :] = own_odd_ref[i, j]
-            ext[k, strip(2), :] = own_even_ref[i, j]
-            ext[k, strip(3), :] = even_ref[1 - row_parity, i, j]
+            ext[k, strip_rows(0), :] = odd_ref[i, j]
+            ext[k, strip_rows(1), :] = own_odd_ref[i, j]
+            ext[k, strip_rows(2), :] = own_even_ref[i, j]
+            ext[k, strip_rows(3), :] = even_ref[1 - row_parity, i, j]
     lane = lax.broadcasted_iota(jnp.int32, (N + 8, N), 1)
-    live = counts_ref[0, 0]
+    live = jnp.max(scal_ref[4:5, :])
     sub = lax.broadcasted_iota(jnp.int32, (N // 8, 8, N), 1)
     rows, turns, masks, wraps = [], [], [], []
     for slot in range(2):
-        row = positions_ref[0, 0, 0, slot] - lax.axis_index("row") * N + H
-        column = positions_ref[0, 0, 1, slot] - lax.axis_index("col") * N + H
+        row = jnp.max(scal_ref[slot : slot + 1, :])
+        column = jnp.max(scal_ref[2 + slot : 3 + slot, :])
         turn = jnp.where(column < H, column + H, column - H)
         masks.append((lane >= turn) != (column < H))
         rows.append(row)
@@ -181,8 +200,8 @@
         return out[:, :N], out[:, N:]
 
     probe_re, probe_im = twice(probe_ref[0]), twice(probe_ref[1])
-    k_re = jnp.concatenate([kernel_ref[0], kernel_ref[0]], axis=1)
-    k_im = jnp.concatenate([kernel_ref[1], kernel_ref[1]], axis=1)
+    k_re = jnp.concatenate([kernel_re_ref[...]] * 2, axis=1)
+    k_im = jnp.concatenate([kernel_im_ref[...]] * 2, axis=1)
     t_re, t_im = both(0)
     w_re = t_re * probe_re - t_im * probe_im
     w_im = t_re * probe_im + t_im * probe_re
@@ -229,8 +248,8 @@
         for j in range(2):
             k = 2 * i + j
             mid_ref[i, j] = acc[k, H : 3 * H, :]
-            to_even_ref[i, j] = acc[k, strip(3), :]
-            to_odd_ref[i, j] = acc[k, strip(0), :]
+            to_even_ref[i, j] = acc[k, strip_rows(3), :]
+            to_odd_ref[i, j] = acc[k, strip_rows(0), :]
 
 
 def fold_rows_kernel(mid_ref, row_even_ref, row_odd_ref, own_ref, even_ref, odd_ref):
@@ -255,14 +274,14 @@
             out_ref[i, j, H:, :] = own_ref[i, j, H:, :] + bottom
 
 
-def call(body, shapes, *operands, specs=None, scratch=(), name=None, flops=0):
-    outs = [jax.ShapeDtypeStruct(shape, F32) for shape in shapes]
+def call(body, shapes, *operands, kinds=None, scratch=(), name=None, flops=0):
+    kinds = kinds or [F32] * len(shapes)
     size = 4 * sum(math.prod(s) for s in shapes) + sum(4 * o.size for o in operands)
     return pl.pallas_call(
         body,
-        out_shape=outs,
-        in_specs=specs or [VMEM] * len(operands),
-        out_specs=[VMEM] * len(outs),
+        out_shape=[jax.ShapeDtypeStruct(*each) for each in zip(shapes, kinds)],
+        in_specs=[VMEM] * len(operands),
+        out_specs=[VMEM] * len(shapes),
         scratch_shapes=list(scratch),
         compiler_params=pltpu.CompilerParams(vmem_limit_bytes=32 * 2**20),
         cost_estimate=pl.CostEstimate(flops=flops, bytes_accessed=size, transcendentals=0),
@@ -283,25 +302,28 @@
     packed = (2, 2, H, N)
     strip = (2, 2, H, 2 * N)
     tile = (2, 2, N, N)
-    kernel = jnp.stack([jnp.cos(prop_phase), jnp.sin(prop_phase)])
     tables = jnp.asarray(dft_tables())
 
     strips = call(pack_kernel, [packed] * 2, obj_slices, name="pack_columns")
     strips = exchange(*strips, "col")
     own = call(rows_kernel, [strip] * 2, obj_slices, *strips, name="pack_rows")
-    strips = exchange(*own, "row")
+    even, odd = exchange(*own, "row")
+    even, *rest = lax.optimization_barrier((even, prop_phase, positions, counts))
+    kernel_re, kernel_im, scalars = call(
+        prepare_kernel, [(N, N), (N, N), (8, N)], *rest, kinds=[F32, F32, jnp.int32], name="prepare"
+    )
     mid, *strips = call(
         main_kernel,
         [(2, 2, N, 2 * N), strip, strip],
-        positions,
-        counts,
+        scalars,
         *own,
-        *strips,
+        even,
+        odd,
         probe_wave,
-        kernel,
+        kernel_re,
+        kernel_im,
         measured[0, 0],
         tables,
-        specs=[SMEM] * 2 + [VMEM] * 8,
         scratch=[pltpu.VMEM((4, 2 * N, 2 * N), F32), pltpu.VMEM((4, 2 * N, 2 * N), F32)],
         name="window_gradients",
         flops=36 * 2 * 256**3,

time: 59.1 us -> 56.9 us (0.963)
  Pallas kernels: 5.91 us -> 4.69 us
  waiting for transfers between devices: 8.09 us -> 7.16 us
    pallas_call x5 -> x6, Pallas kernels: 5.91 us -> 4.69 us  [call(): pl.pallas_call(body, out_shape=[jax.ShapeDtypeStruct(*each) for each in z...]
    ppermute x4, waiting for transfers between devices: 8.09 us -> 7.16 us  [exchange(): odd = lax.ppermute(odd, axis, pairs + [(b, a) for a, b in pairs])]
  transfers between devices with their start and end apart: 4 -> 4, of which waited for: 2 -> 2; matrix products, arithmetic and copies ran while one was open for 0% -> 0% of each run, Pallas kernels for 0% -> 1%
where the time goes in v3:
time: 56.9 us; the launch traced here: 56.6 us
  starting transfers between devices  26.1 us (46%)
  blocking collectives  16.2 us (28%)
  waiting for transfers between devices  7.16 us (13%)
  Pallas kernels  4.69 us (8%)
  local copies, waits for them, and re-layouts  1.65 us (3%)
  between operations  0.75 us (1%)
    ppermute x4, starting transfers between devices, exchange(): odd = lax.ppermute(odd, axis, pairs + [(b, a) for a, b in pairs])  26.1 us
    all_gather x4, blocking collectives, exchange(): even = lax.all_gather(even, axis, axis_index_groups=groups)  16.2 us
    ppermute x4, waiting for transfers between devices, exchange(): odd = lax.ppermute(odd, axis, pairs + [(b, a) for a, b in pairs])  7.16 us
    pallas_call x6, Pallas kernels, call(): pl.pallas_call(body, out_shape=[jax.ShapeDtypeStruct(*each) for each in z...  4.69 us
    unnamed x12, local copies, waits for them, and re-layouts  1.65 us
  transfers between devices with their start and end apart: 4, of which 2 were waited for; matrix products, arithmetic and copies ran while one was open for 0% of the time, Pallas kernels for 1%

profile of v3, /device:TPU:38, one launch (start us, length us, event | category | flops | bytes accessed | tf_op | source)
XLA Modules:
  0.0 56.6 jit_solution(8641825386503294441)
XLA Ops:
  0.0 0.9 %copy-done = f32[2,2,128,128]{3,2,1,0:T(8,128)S(1)} copy-done((f32[2,2,128,128]{3,2,1,0:T(8,128)S(1)}, f32[2,2,128,128]{3,2,1,0:T(8,128)}, u32[]{:S(2)}) %copy-start) | copy-done | bytes 262168
  1.0 0.1 pack_columns.1
  1.1 18.5 %collective-permute-start = (f32[2,2,64,128]{3,2,1,0:T(8,128)S(1)}, f32[2,2,64,128]{3,2,1,0:T(8,128)S(1)}, u32[]{:S(2)}, u32[]{:S(2)}) collective-permute-start(f32[2,2,64,128]{3,2,1,0:T(8,128)S(1)} %get-tuple-element.23), channel_id=1, source_target_pairs={{1,2},{3,4},{5,6},{7,8},{9,10},{11,12},{13,14},{15,16},{17,18},{19... | collective-permute-start | bytes 393224 | tf_op jit(solution)/shard_map/ppermute | solution.py:295
  19.6 5.6 %all-gather = f32[4,2,64,128]{3,2,1,0:T(8,128)S(1)} all-gather(f32[2,2,64,128]{3,2,1,0:T(8,128)S(1)} %get-tuple-element.22), channel_id=2, replica_groups={{0,1},{2,3},{4,5},{6,7},{8,9},{10,11},{12,13},{14,15},{16,17},{18,19},{..., dimensions={0}, use_global_device_ids=true | all-gather | bytes 393216 | tf_op jit(solution)/shard_map/all_gather | solution.py:297
  25.2 0.0 collective-permute-done.odd_ref
  25.2 0.1 pack_rows.1
  25.3 2.1 %collective-permute-start.1 = (f32[2,2,64,256]{3,2,1,0:T(8,128)S(1)}, f32[2,2,64,256]{3,2,1,0:T(8,128)S(1)}, u32[]{:S(2)}, u32[]{:S(2)}) collective-permute-start(f32[2,2,64,256]{3,2,1,0:T(8,128)S(1)} %get-tuple-element.29.own_odd_ref), channel_id=1, source_target_pairs={{64,128},{192,256},{320,384},{448,512},{576,640},{704,768},{832,89... | collective-permute-start | bytes 786440 | tf_op jit(solution)/shard_map/ppermute | solution.py:295
  28.0 0.0 copy-start.1
  28.0 0.0 copy-start.3
  28.1 0.0 copy-start.4
  28.1 2.7 %all-gather.1 = f32[4,2,64,256]{3,2,1,0:T(8,128)S(1)} all-gather(f32[2,2,64,256]{3,2,1,0:T(8,128)S(1)} %get-tuple-element.24.own_even_ref), channel_id=3, replica_groups={{0,64},{128,192},{256,320},{384,448},{512,576},{640,704},{768,832},{896..., dimensions={0}, use_global_device_ids=true | all-gather | bytes 786432 | tf_op jit(solution)/shard_map/all_gather | solution.py:297
  30.8 0.7 %copy-done.2 = s32[1,1,2,2]{3,2,1,0:T(2,128)S(1)} copy-done((s32[1,1,2,2]{3,2,1,0:T(2,128)S(1)}, s32[1,1,2,2]{3,2,1,0:T(2,128)}, u32[]{:S(2)}) %copy-start.2) | copy-done | bytes 40
  31.5 0.4 prepare.1
  31.9 2.5 %collective-permute-done.1.odd_ref = f32[2,2,64,256]{3,2,1,0:T(8,128)S(1)} collective-permute-done((f32[2,2,64,256]{3,2,1,0:T(8,128)S(1)}, f32[2,2,64,256]{3,2,1,0:T(8,128)S(1)}, u32[]{:S(2)}, u32[]{:S(2)}) %collective-permute-start.1) | collective-permute-done | bytes 262176 | tf_op jit(solution)/shard_map/ppermute | solution.py:295
  34.4 0.0 copy-done.4
  34.4 3.1 %window_gradients.1 = (f32[2,2,128,256]{3,2,1,0:T(8,128)S(1)}, f32[2,2,64,256]{3,2,1,0:T(8,128)S(1)}, f32[2,2,64,256]{3,2,1,0:T(8,128)S(1)}) custom-call(s32[8,128]{1,0:T(8,128)S(1)} %get-tuple-element.28.scal_ref, f32[2,2,64,256]{3,2,1,0:T(8,128)S(1)} %get-tuple-element.24.own_even_ref, f32[2,2,64,256]{3,2,1,0:T(8,128)S(1)} %get-tuple-element.29.own_odd_ref, ...), custom_call_target="tpu_custom_call" | custom-call | flops 1207959552 | bytes 3805184 | tf_op jit(solution)/shard_map/window_gradients/pallas_call | solution.py:280
  37.5 2.0 %collective-permute-start.2 = (f32[2,2,64,256]{3,2,1,0:T(8,128)S(1)}, f32[2,2,64,256]{3,2,1,0:T(8,128)S(1)}, u32[]{:S(2)}, u32[]{:S(2)}) collective-permute-start(f32[2,2,64,256]{3,2,1,0:T(8,128)S(1)} %get-tuple-element.35), channel_id=1, source_target_pairs={{64,128},{192,256},{320,384},{448,512},{576,640},{704,768},{832,89... | collective-permute-start | bytes 786440 | tf_op jit(solution)/shard_map/ppermute | solution.py:295
  39.5 2.2 %all-gather.2 = f32[4,2,64,256]{3,2,1,0:T(8,128)S(1)} all-gather(f32[2,2,64,256]{3,2,1,0:T(8,128)S(1)} %get-tuple-element.34), channel_id=4, replica_groups={{0,64},{128,192},{256,320},{384,448},{512,576},{640,704},{768,832},{896..., dimensions={0}, use_global_device_ids=true | all-gather | bytes 786432 | tf_op jit(solution)/shard_map/all_gather | solution.py:297
  41.7 4.7 %collective-permute-done.2.row_odd_ref = f32[2,2,64,256]{3,2,1,0:T(8,128)S(1)} collective-permute-done((f32[2,2,64,256]{3,2,1,0:T(8,128)S(1)}, f32[2,2,64,256]{3,2,1,0:T(8,128)S(1)}, u32[]{:S(2)}, u32[]{:S(2)}) %collective-permute-start.2) | collective-permute-done | bytes 262176 | tf_op jit(solution)/shard_map/ppermute | solution.py:295
  46.4 0.1 fold_rows.1
  46.5 3.6 %collective-permute-start.3 = (f32[2,2,64,128]{3,2,1,0:T(8,128)S(1)}, f32[2,2,64,128]{3,2,1,0:T(8,128)S(1)}, u32[]{:S(2)}, u32[]{:S(2)}) collective-permute-start(f32[2,2,64,128]{3,2,1,0:T(8,128)S(1)} %get-tuple-element.38), channel_id=1, source_target_pairs={{1,2},{3,4},{5,6},{7,8},{9,10},{11,12},{13,14},{15,16},{17,18},{19... | collective-permute-start | bytes 393224 | tf_op jit(solution)/shard_map/ppermute | solution.py:295
  50.1 5.6 %all-gather.3 = f32[4,2,64,128]{3,2,1,0:T(8,128)S(1)} all-gather(f32[2,2,64,128]{3,2,1,0:T(8,128)S(1)} %get-tuple-element.37), channel_id=5, replica_groups={{0,1},{2,3},{4,5},{6,7},{8,9},{10,11},{12,13},{14,15},{16,17},{18,19},{..., dimensions={0}, use_global_device_ids=true | all-gather | bytes 393216 | tf_op jit(solution)/shard_map/all_gather | solution.py:297
  55.8 0.0 collective-permute-done.3.odd_ref
  55.8 0.8 %fold_columns.1 = f32[2,2,128,128]{3,2,1,0:T(8,128)} custom-call(f32[2,2,128,128]{3,2,1,0:T(8,128)S(1)} %get-tuple-element.36.own_ref, f32[2,2,2,64,128]{4,3,2,1,0:T(8,128)S(1)} %bitcast.6, f32[2,2,64,128]{3,2,1,0:T(8,128)S(1)} %collective-permute-done.3.odd_ref), custom_call_target="tpu_custom_call" | custom-call | bytes 917504 | tf_op jit(solution)/shard_map/fold_columns/pallas_call | solution.py:280
  (6 shorter events, 0.0 us)
Async XLA Ops:
  0.0 0.9 %copy-start = (f32[2,2,128,128]{3,2,1,0:T(8,128)S(1)}, f32[2,2,128,128]{3,2,1,0:T(8,128)}, u32[]{:S(2)}) copy-start(f32[2,2,128,128]{3,2,1,0:T(8,128)} %obj_ref.3) | copy-start | bytes 786436
  1.1 24.1 %collective-permute-start = (f32[2,2,64,128]{3,2,1,0:T(8,128)S(1)}, f32[2,2,64,128]{3,2,1,0:T(8,128)S(1)}, u32[]{:S(2)}, u32[]{:S(2)}) collective-permute-start(f32[2,2,64,128]{3,2,1,0:T(8,128)S(1)} %get-tuple-element.23), channel_id=1, source_target_pairs={{1,2},{3,4},{5,6},{7,8},{9,10},{11,12},{13,14},{15,16},{17,18},{19... | collective-permute-start | bytes 393224 | tf_op jit(solution)/shard_map/ppermute | solution.py:295
  25.2 9.2 %copy-start.5 = (bf16[4,256,256]{2,1,0:T(8,128)(2,1)S(1)}, bf16[4,256,256]{2,1,0:T(8,128)(2,1)}, u32[]{:S(2)}) copy-start(bf16[4,256,256]{2,1,0:T(8,128)(2,1)} %constant.2.clone.table_ref) | copy-start | bytes 1572868
  25.3 9.0 %collective-permute-start.1 = (f32[2,2,64,256]{3,2,1,0:T(8,128)S(1)}, f32[2,2,64,256]{3,2,1,0:T(8,128)S(1)}, u32[]{:S(2)}, u32[]{:S(2)}) collective-permute-start(f32[2,2,64,256]{3,2,1,0:T(8,128)S(1)} %get-tuple-element.29.own_odd_ref), channel_id=1, source_target_pairs={{64,128},{192,256},{320,384},{448,512},{576,640},{704,768},{832,89... | collective-permute-start | bytes 786440 | tf_op jit(solution)/shard_map/ppermute | solution.py:295
  28.0 2.8 %copy-start.1 = (f32[128,128]{1,0:T(8,128)S(1)}, f32[128,128]{1,0:T(8,128)}, u32[]{:S(2)}) copy-start(f32[128,128]{1,0:T(8,128)} %phase_ref) | copy-start | bytes 196612
  28.0 6.3 %copy-start.3 = (f32[2,128,128]{2,1,0:T(8,128)S(1)}, f32[2,128,128]{2,1,0:T(8,128)}, u32[]{:S(2)}) copy-start(f32[2,128,128]{2,1,0:T(8,128)} %probe_ref.1) | copy-start | bytes 393220
  28.1 6.3 %copy-start.4 = (f32[1,1,2,128,128]{4,3,2,1,0:T(8,128)S(1)}, f32[1,1,2,128,128]{4,3,2,1,0:T(8,128)}, u32[]{:S(2)}) copy-start(f32[1,1,2,128,128]{4,3,2,1,0:T(8,128)} %param.10) | copy-start | bytes 393220
  30.8 0.7 %copy-start.2 = (s32[1,1,2,2]{3,2,1,0:T(2,128)S(1)}, s32[1,1,2,2]{3,2,1,0:T(2,128)}, u32[]{:S(2)}) copy-start(s32[1,1,2,2]{3,2,1,0:T(2,128)} %positions_ref) | copy-start | bytes 52
  37.5 8.9 %collective-permute-start.2 = (f32[2,2,64,256]{3,2,1,0:T(8,128)S(1)}, f32[2,2,64,256]{3,2,1,0:T(8,128)S(1)}, u32[]{:S(2)}, u32[]{:S(2)}) collective-permute-start(f32[2,2,64,256]{3,2,1,0:T(8,128)S(1)} %get-tuple-element.35), channel_id=1, source_target_pairs={{64,128},{192,256},{320,384},{448,512},{576,640},{704,768},{832,89... | collective-permute-start | bytes 786440 | tf_op jit(solution)/shard_map/ppermute | solution.py:295
  46.5 9.2 %collective-permute-start.3 = (f32[2,2,64,128]{3,2,1,0:T(8,128)S(1)}, f32[2,2,64,128]{3,2,1,0:T(8,128)S(1)}, u32[]{:S(2)}, u32[]{:S(2)}) collective-permute-start(f32[2,2,64,128]{3,2,1,0:T(8,128)S(1)} %get-tuple-element.38), channel_id=1, source_target_pairs={{1,2},{3,4},{5,6},{7,8},{9,10},{11,12},{13,14},{15,16},{17,18},{19... | collective-permute-start | bytes 393224 | tf_op jit(solution)/shard_map/ppermute | solution.py:295

commit v4 on v3

--- a/solution.py
+++ b/solution.py
@@ -83,9 +83,10 @@
 def from_right(value, high, low):
     v_high, v_low = split(value)
     out = []
-    for slot in (slice(0, N), slice(N, 2 * N)):
+    for q in range(4):
+        slot = slice(q * H, (q + 1) * H)
         both = dot(jnp.concatenate([v_high[slot], v_low[slot]], axis=0), high)
-        out.append(both[:N] + (both[N:] + dot(v_high[slot], low)))
+        out.append(both[:H] + (both[H:] + dot(v_high[slot], low)))
     return jnp.concatenate(out, axis=0)
 
 

time: 56.9 us -> 56.7 us (level)
  no operation moved by 1% of the time
where the time goes in v4:
time: 56.7 us; the launch traced here: 56.5 us
  starting transfers between devices  26.2 us (46%)
  blocking collectives  16.2 us (29%)
  waiting for transfers between devices  7.14 us (13%)
  Pallas kernels  4.57 us (8%)
  local copies, waits for them, and re-layouts  1.65 us (3%)
  between operations  0.75 us (1%)
    ppermute x4, starting transfers between devices, exchange(): odd = lax.ppermute(odd, axis, pairs + [(b, a) for a, b in pairs])  26.2 us
    all_gather x4, blocking collectives, exchange(): even = lax.all_gather(even, axis, axis_index_groups=groups)  16.2 us
    ppermute x4, waiting for transfers between devices, exchange(): odd = lax.ppermute(odd, axis, pairs + [(b, a) for a, b in pairs])  7.14 us
    pallas_call x6, Pallas kernels, call(): pl.pallas_call(body, out_shape=[jax.ShapeDtypeStruct(*each) for each in z...  4.57 us
    unnamed x12, local copies, waits for them, and re-layouts  1.65 us
  transfers between devices with their start and end apart: 4, of which 2 were waited for; matrix products, arithmetic and copies ran while one was open for 0% of the time, Pallas kernels for 1%

profile of v4, /device:TPU:38, one launch (start us, length us, event | category | flops | bytes accessed | tf_op | source)
XLA Modules:
  0.0 56.5 jit_solution(1670212274054425073)
XLA Ops:
  0.0 0.9 %copy-done = f32[2,2,128,128]{3,2,1,0:T(8,128)S(1)} copy-done((f32[2,2,128,128]{3,2,1,0:T(8,128)S(1)}, f32[2,2,128,128]{3,2,1,0:T(8,128)}, u32[]{:S(2)}) %copy-start) | copy-done | bytes 262168
  1.0 0.1 pack_columns.1
  1.1 18.5 %collective-permute-start = (f32[2,2,64,128]{3,2,1,0:T(8,128)S(1)}, f32[2,2,64,128]{3,2,1,0:T(8,128)S(1)}, u32[]{:S(2)}, u32[]{:S(2)}) collective-permute-start(f32[2,2,64,128]{3,2,1,0:T(8,128)S(1)} %get-tuple-element.23), channel_id=1, source_target_pairs={{1,2},{3,4},{5,6},{7,8},{9,10},{11,12},{13,14},{15,16},{17,18},{19... | collective-permute-start | bytes 393224 | tf_op jit(solution)/shard_map/ppermute | solution.py:296
  19.6 5.6 %all-gather = f32[4,2,64,128]{3,2,1,0:T(8,128)S(1)} all-gather(f32[2,2,64,128]{3,2,1,0:T(8,128)S(1)} %get-tuple-element.22), channel_id=2, replica_groups={{0,1},{2,3},{4,5},{6,7},{8,9},{10,11},{12,13},{14,15},{16,17},{18,19},{..., dimensions={0}, use_global_device_ids=true | all-gather | bytes 393216 | tf_op jit(solution)/shard_map/all_gather | solution.py:298
  25.2 0.0 collective-permute-done.odd_ref
  25.2 0.1 pack_rows.1
  25.3 2.1 %collective-permute-start.1 = (f32[2,2,64,256]{3,2,1,0:T(8,128)S(1)}, f32[2,2,64,256]{3,2,1,0:T(8,128)S(1)}, u32[]{:S(2)}, u32[]{:S(2)}) collective-permute-start(f32[2,2,64,256]{3,2,1,0:T(8,128)S(1)} %get-tuple-element.29.own_odd_ref), channel_id=1, source_target_pairs={{64,128},{192,256},{320,384},{448,512},{576,640},{704,768},{832,89... | collective-permute-start | bytes 786440 | tf_op jit(solution)/shard_map/ppermute | solution.py:296
  28.0 0.0 copy-start.1
  28.0 0.0 copy-start.3
  28.1 0.0 copy-start.4
  28.1 2.7 %all-gather.1 = f32[4,2,64,256]{3,2,1,0:T(8,128)S(1)} all-gather(f32[2,2,64,256]{3,2,1,0:T(8,128)S(1)} %get-tuple-element.24.own_even_ref), channel_id=3, replica_groups={{0,64},{128,192},{256,320},{384,448},{512,576},{640,704},{768,832},{896..., dimensions={0}, use_global_device_ids=true | all-gather | bytes 786432 | tf_op jit(solution)/shard_map/all_gather | solution.py:298
  30.8 0.0 copy-done.1
  30.8 0.7 %copy-done.2 = s32[1,1,2,2]{3,2,1,0:T(2,128)S(1)} copy-done((s32[1,1,2,2]{3,2,1,0:T(2,128)S(1)}, s32[1,1,2,2]{3,2,1,0:T(2,128)}, u32[]{:S(2)}) %copy-start.2) | copy-done | bytes 40
  31.5 0.4 prepare.1
  31.9 2.5 %collective-permute-done.1.odd_ref = f32[2,2,64,256]{3,2,1,0:T(8,128)S(1)} collective-permute-done((f32[2,2,64,256]{3,2,1,0:T(8,128)S(1)}, f32[2,2,64,256]{3,2,1,0:T(8,128)S(1)}, u32[]{:S(2)}, u32[]{:S(2)}) %collective-permute-start.1) | collective-permute-done | bytes 262176 | tf_op jit(solution)/shard_map/ppermute | solution.py:296
  34.4 3.0 %window_gradients.1 = (f32[2,2,128,256]{3,2,1,0:T(8,128)S(1)}, f32[2,2,64,256]{3,2,1,0:T(8,128)S(1)}, f32[2,2,64,256]{3,2,1,0:T(8,128)S(1)}) custom-call(s32[8,128]{1,0:T(8,128)S(1)} %get-tuple-element.28.scal_ref, f32[2,2,64,256]{3,2,1,0:T(8,128)S(1)} %get-tuple-element.24.own_even_ref, f32[2,2,64,256]{3,2,1,0:T(8,128)S(1)} %get-tuple-element.29.own_odd_ref, ...), custom_call_target="tpu_custom_call" | custom-call | flops 1207959552 | bytes 3805184 | tf_op jit(solution)/shard_map/window_gradients/pallas_call | solution.py:281
  37.4 2.0 %collective-permute-start.2 = (f32[2,2,64,256]{3,2,1,0:T(8,128)S(1)}, f32[2,2,64,256]{3,2,1,0:T(8,128)S(1)}, u32[]{:S(2)}, u32[]{:S(2)}) collective-permute-start(f32[2,2,64,256]{3,2,1,0:T(8,128)S(1)} %get-tuple-element.35), channel_id=1, source_target_pairs={{64,128},{192,256},{320,384},{448,512},{576,640},{704,768},{832,89... | collective-permute-start | bytes 786440 | tf_op jit(solution)/shard_map/ppermute | solution.py:296
  39.4 2.2 %all-gather.2 = f32[4,2,64,256]{3,2,1,0:T(8,128)S(1)} all-gather(f32[2,2,64,256]{3,2,1,0:T(8,128)S(1)} %get-tuple-element.34), channel_id=4, replica_groups={{0,64},{128,192},{256,320},{384,448},{512,576},{640,704},{768,832},{896..., dimensions={0}, use_global_device_ids=true | all-gather | bytes 786432 | tf_op jit(solution)/shard_map/all_gather | solution.py:298
  41.6 4.7 %collective-permute-done.2.row_odd_ref = f32[2,2,64,256]{3,2,1,0:T(8,128)S(1)} collective-permute-done((f32[2,2,64,256]{3,2,1,0:T(8,128)S(1)}, f32[2,2,64,256]{3,2,1,0:T(8,128)S(1)}, u32[]{:S(2)}, u32[]{:S(2)}) %collective-permute-start.2) | collective-permute-done | bytes 262176 | tf_op jit(solution)/shard_map/ppermute | solution.py:296
  46.3 0.1 fold_rows.1
  46.4 3.6 %collective-permute-start.3 = (f32[2,2,64,128]{3,2,1,0:T(8,128)S(1)}, f32[2,2,64,128]{3,2,1,0:T(8,128)S(1)}, u32[]{:S(2)}, u32[]{:S(2)}) collective-permute-start(f32[2,2,64,128]{3,2,1,0:T(8,128)S(1)} %get-tuple-element.38), channel_id=1, source_target_pairs={{1,2},{3,4},{5,6},{7,8},{9,10},{11,12},{13,14},{15,16},{17,18},{19... | collective-permute-start | bytes 393224 | tf_op jit(solution)/shard_map/ppermute | solution.py:296
  50.0 5.6 %all-gather.3 = f32[4,2,64,128]{3,2,1,0:T(8,128)S(1)} all-gather(f32[2,2,64,128]{3,2,1,0:T(8,128)S(1)} %get-tuple-element.37), channel_id=5, replica_groups={{0,1},{2,3},{4,5},{6,7},{8,9},{10,11},{12,13},{14,15},{16,17},{18,19},{..., dimensions={0}, use_global_device_ids=true | all-gather | bytes 393216 | tf_op jit(solution)/shard_map/all_gather | solution.py:298
  55.6 0.0 collective-permute-done.3.odd_ref
  55.7 0.8 %fold_columns.1 = f32[2,2,128,128]{3,2,1,0:T(8,128)} custom-call(f32[2,2,128,128]{3,2,1,0:T(8,128)S(1)} %get-tuple-element.36.own_ref, f32[2,2,2,64,128]{4,3,2,1,0:T(8,128)S(1)} %bitcast.6, f32[2,2,64,128]{3,2,1,0:T(8,128)S(1)} %collective-permute-done.3.odd_ref), custom_call_target="tpu_custom_call" | custom-call | bytes 917504 | tf_op jit(solution)/shard_map/fold_columns/pallas_call | solution.py:281
  (6 shorter events, 0.0 us)
Async XLA Ops:
  0.0 0.9 %copy-start = (f32[2,2,128,128]{3,2,1,0:T(8,128)S(1)}, f32[2,2,128,128]{3,2,1,0:T(8,128)}, u32[]{:S(2)}) copy-start(f32[2,2,128,128]{3,2,1,0:T(8,128)} %obj_ref.3) | copy-start | bytes 786436
  1.1 24.1 %collective-permute-start = (f32[2,2,64,128]{3,2,1,0:T(8,128)S(1)}, f32[2,2,64,128]{3,2,1,0:T(8,128)S(1)}, u32[]{:S(2)}, u32[]{:S(2)}) collective-permute-start(f32[2,2,64,128]{3,2,1,0:T(8,128)S(1)} %get-tuple-element.23), channel_id=1, source_target_pairs={{1,2},{3,4},{5,6},{7,8},{9,10},{11,12},{13,14},{15,16},{17,18},{19... | collective-permute-start | bytes 393224 | tf_op jit(solution)/shard_map/ppermute | solution.py:296
  25.2 9.2 %copy-start.5 = (bf16[4,256,256]{2,1,0:T(8,128)(2,1)S(1)}, bf16[4,256,256]{2,1,0:T(8,128)(2,1)}, u32[]{:S(2)}) copy-start(bf16[4,256,256]{2,1,0:T(8,128)(2,1)} %constant.2.clone.table_ref) | copy-start | bytes 1572868
  25.3 9.0 %collective-permute-start.1 = (f32[2,2,64,256]{3,2,1,0:T(8,128)S(1)}, f32[2,2,64,256]{3,2,1,0:T(8,128)S(1)}, u32[]{:S(2)}, u32[]{:S(2)}) collective-permute-start(f32[2,2,64,256]{3,2,1,0:T(8,128)S(1)} %get-tuple-element.29.own_odd_ref), channel_id=1, source_target_pairs={{64,128},{192,256},{320,384},{448,512},{576,640},{704,768},{832,89... | collective-permute-start | bytes 786440 | tf_op jit(solution)/shard_map/ppermute | solution.py:296
  28.0 2.8 %copy-start.1 = (f32[128,128]{1,0:T(8,128)S(1)}, f32[128,128]{1,0:T(8,128)}, u32[]{:S(2)}) copy-start(f32[128,128]{1,0:T(8,128)} %phase_ref) | copy-start | bytes 196612
  28.0 6.3 %copy-start.3 = (f32[2,128,128]{2,1,0:T(8,128)S(1)}, f32[2,128,128]{2,1,0:T(8,128)}, u32[]{:S(2)}) copy-start(f32[2,128,128]{2,1,0:T(8,128)} %probe_ref.1) | copy-start | bytes 393220
  28.1 6.3 %copy-start.4 = (f32[1,1,2,128,128]{4,3,2,1,0:T(8,128)S(1)}, f32[1,1,2,128,128]{4,3,2,1,0:T(8,128)}, u32[]{:S(2)}) copy-start(f32[1,1,2,128,128]{4,3,2,1,0:T(8,128)} %param.10) | copy-start | bytes 393220
  30.8 0.7 %copy-start.2 = (s32[1,1,2,2]{3,2,1,0:T(2,128)S(1)}, s32[1,1,2,2]{3,2,1,0:T(2,128)}, u32[]{:S(2)}) copy-start(s32[1,1,2,2]{3,2,1,0:T(2,128)} %positions_ref) | copy-start | bytes 52
  37.4 8.9 %collective-permute-start.2 = (f32[2,2,64,256]{3,2,1,0:T(8,128)S(1)}, f32[2,2,64,256]{3,2,1,0:T(8,128)S(1)}, u32[]{:S(2)}, u32[]{:S(2)}) collective-permute-start(f32[2,2,64,256]{3,2,1,0:T(8,128)S(1)} %get-tuple-element.35), channel_id=1, source_target_pairs={{64,128},{192,256},{320,384},{448,512},{576,640},{704,768},{832,89... | collective-permute-start | bytes 786440 | tf_op jit(solution)/shard_map/ppermute | solution.py:296
  46.4 9.2 %collective-permute-start.3 = (f32[2,2,64,128]{3,2,1,0:T(8,128)S(1)}, f32[2,2,64,128]{3,2,1,0:T(8,128)S(1)}, u32[]{:S(2)}, u32[]{:S(2)}) collective-permute-start(f32[2,2,64,128]{3,2,1,0:T(8,128)S(1)} %get-tuple-element.38), channel_id=1, source_target_pairs={{1,2},{3,4},{5,6},{7,8},{9,10},{11,12},{13,14},{15,16},{17,18},{19... | collective-permute-start | bytes 393224 | tf_op jit(solution)/shard_map/ppermute | solution.py:296

commit v5 on v4

--- a/solution.py
+++ b/solution.py
@@ -309,7 +309,8 @@
     strips = exchange(*strips, "col")
     own = call(rows_kernel, [strip] * 2, obj_slices, *strips, name="pack_rows")
     even, odd = exchange(*own, "row")
-    even, *rest = lax.optimization_barrier((even, prop_phase, positions, counts))
+    even, prop_phase = lax.optimization_barrier((even, prop_phase))
+    rest = (prop_phase, positions, counts)
     kernel_re, kernel_im, scalars = call(
         prepare_kernel, [(N, N), (N, N), (8, N)], *rest, kinds=[F32, F32, jnp.int32], name="prepare"
     )

time: 56.7 us -> 56.7 us (level)
  no operation moved by 1% of the time
where the time goes in v5:
time: 56.7 us; the launch traced here: 56.5 us
  starting transfers between devices  26.2 us (46%)
  blocking collectives  16.2 us (29%)
  waiting for transfers between devices  7.15 us (13%)
  Pallas kernels  4.58 us (8%)
  local copies, waits for them, and re-layouts  1.65 us (3%)
  between operations  0.75 us (1%)
    ppermute x4, starting transfers between devices, exchange(): odd = lax.ppermute(odd, axis, pairs + [(b, a) for a, b in pairs])  26.2 us
    all_gather x4, blocking collectives, exchange(): even = lax.all_gather(even, axis, axis_index_groups=groups)  16.2 us
    ppermute x4, waiting for transfers between devices, exchange(): odd = lax.ppermute(odd, axis, pairs + [(b, a) for a, b in pairs])  7.15 us
    pallas_call x6, Pallas kernels, call(): pl.pallas_call(body, out_shape=[jax.ShapeDtypeStruct(*each) for each in z...  4.58 us
    unnamed x12, local copies, waits for them, and re-layouts  1.65 us
  transfers between devices with their start and end apart: 4, of which 2 were waited for; matrix products, arithmetic and copies ran while one was open for 0% of the time, Pallas kernels for 1%

profile of v5, /device:TPU:38, one launch (start us, length us, event | category | flops | bytes accessed | tf_op | source)
XLA Modules:
  0.0 56.5 jit_solution(1670212274054425073)
XLA Ops:
  0.0 0.9 %copy-done = f32[2,2,128,128]{3,2,1,0:T(8,128)S(1)} copy-done((f32[2,2,128,128]{3,2,1,0:T(8,128)S(1)}, f32[2,2,128,128]{3,2,1,0:T(8,128)}, u32[]{:S(2)}) %copy-start) | copy-done | bytes 262168
  1.0 0.1 pack_columns.1
  1.1 18.5 %collective-permute-start = (f32[2,2,64,128]{3,2,1,0:T(8,128)S(1)}, f32[2,2,64,128]{3,2,1,0:T(8,128)S(1)}, u32[]{:S(2)}, u32[]{:S(2)}) collective-permute-start(f32[2,2,64,128]{3,2,1,0:T(8,128)S(1)} %get-tuple-element.21), channel_id=1, source_target_pairs={{1,2},{3,4},{5,6},{7,8},{9,10},{11,12},{13,14},{15,16},{17,18},{19... | collective-permute-start | bytes 393224 | tf_op jit(solution)/shard_map/ppermute | solution.py:296
  19.6 5.6 %all-gather = f32[4,2,64,128]{3,2,1,0:T(8,128)S(1)} all-gather(f32[2,2,64,128]{3,2,1,0:T(8,128)S(1)} %get-tuple-element.20), channel_id=2, replica_groups={{0,1},{2,3},{4,5},{6,7},{8,9},{10,11},{12,13},{14,15},{16,17},{18,19},{..., dimensions={0}, use_global_device_ids=true | all-gather | bytes 393216 | tf_op jit(solution)/shard_map/all_gather | solution.py:298
  25.2 0.0 collective-permute-done.odd_ref
  25.2 0.1 pack_rows.1
  25.3 2.1 %collective-permute-start.1 = (f32[2,2,64,256]{3,2,1,0:T(8,128)S(1)}, f32[2,2,64,256]{3,2,1,0:T(8,128)S(1)}, u32[]{:S(2)}, u32[]{:S(2)}) collective-permute-start(f32[2,2,64,256]{3,2,1,0:T(8,128)S(1)} %get-tuple-element.25.own_odd_ref), channel_id=1, source_target_pairs={{64,128},{192,256},{320,384},{448,512},{576,640},{704,768},{832,89... | collective-permute-start | bytes 786440 | tf_op jit(solution)/shard_map/ppermute | solution.py:296
  28.0 0.0 copy-start.1
  28.0 0.0 copy-start.3
  28.1 0.0 copy-start.4
  28.1 2.7 %all-gather.1 = f32[4,2,64,256]{3,2,1,0:T(8,128)S(1)} all-gather(f32[2,2,64,256]{3,2,1,0:T(8,128)S(1)} %get-tuple-element.22.own_even_ref), channel_id=3, replica_groups={{0,64},{128,192},{256,320},{384,448},{512,576},{640,704},{768,832},{896..., dimensions={0}, use_global_device_ids=true | all-gather | bytes 786432 | tf_op jit(solution)/shard_map/all_gather | solution.py:298
  30.8 0.7 %copy-done.2 = s32[1,1,2,2]{3,2,1,0:T(2,128)S(1)} copy-done((s32[1,1,2,2]{3,2,1,0:T(2,128)S(1)}, s32[1,1,2,2]{3,2,1,0:T(2,128)}, u32[]{:S(2)}) %copy-start.2) | copy-done | bytes 40
  31.5 0.4 prepare.1
  31.9 2.5 %collective-permute-done.1.odd_ref = f32[2,2,64,256]{3,2,1,0:T(8,128)S(1)} collective-permute-done((f32[2,2,64,256]{3,2,1,0:T(8,128)S(1)}, f32[2,2,64,256]{3,2,1,0:T(8,128)S(1)}, u32[]{:S(2)}, u32[]{:S(2)}) %collective-permute-start.1) | collective-permute-done | bytes 262176 | tf_op jit(solution)/shard_map/ppermute | solution.py:296
  34.4 0.0 copy-done.4
  34.4 3.0 %window_gradients.1 = (f32[2,2,128,256]{3,2,1,0:T(8,128)S(1)}, f32[2,2,64,256]{3,2,1,0:T(8,128)S(1)}, f32[2,2,64,256]{3,2,1,0:T(8,128)S(1)}) custom-call(s32[8,128]{1,0:T(8,128)S(1)} %get-tuple-element.24.scal_ref, f32[2,2,64,256]{3,2,1,0:T(8,128)S(1)} %get-tuple-element.22.own_even_ref, f32[2,2,64,256]{3,2,1,0:T(8,128)S(1)} %get-tuple-element.25.own_odd_ref, ...), custom_call_target="tpu_custom_call" | custom-call | flops 1207959552 | bytes 3805184 | tf_op jit(solution)/shard_map/window_gradients/pallas_call | solution.py:281
  37.4 2.0 %collective-permute-start.2 = (f32[2,2,64,256]{3,2,1,0:T(8,128)S(1)}, f32[2,2,64,256]{3,2,1,0:T(8,128)S(1)}, u32[]{:S(2)}, u32[]{:S(2)}) collective-permute-start(f32[2,2,64,256]{3,2,1,0:T(8,128)S(1)} %get-tuple-element.31), channel_id=1, source_target_pairs={{64,128},{192,256},{320,384},{448,512},{576,640},{704,768},{832,89... | collective-permute-start | bytes 786440 | tf_op jit(solution)/shard_map/ppermute | solution.py:296
  39.4 2.2 %all-gather.2 = f32[4,2,64,256]{3,2,1,0:T(8,128)S(1)} all-gather(f32[2,2,64,256]{3,2,1,0:T(8,128)S(1)} %get-tuple-element.30), channel_id=4, replica_groups={{0,64},{128,192},{256,320},{384,448},{512,576},{640,704},{768,832},{896..., dimensions={0}, use_global_device_ids=true | all-gather | bytes 786432 | tf_op jit(solution)/shard_map/all_gather | solution.py:298
  41.6 4.7 %collective-permute-done.2.row_odd_ref = f32[2,2,64,256]{3,2,1,0:T(8,128)S(1)} collective-permute-done((f32[2,2,64,256]{3,2,1,0:T(8,128)S(1)}, f32[2,2,64,256]{3,2,1,0:T(8,128)S(1)}, u32[]{:S(2)}, u32[]{:S(2)}) %collective-permute-start.2) | collective-permute-done | bytes 262176 | tf_op jit(solution)/shard_map/ppermute | solution.py:296
  46.3 0.1 fold_rows.1
  46.4 3.6 %collective-permute-start.3 = (f32[2,2,64,128]{3,2,1,0:T(8,128)S(1)}, f32[2,2,64,128]{3,2,1,0:T(8,128)S(1)}, u32[]{:S(2)}, u32[]{:S(2)}) collective-permute-start(f32[2,2,64,128]{3,2,1,0:T(8,128)S(1)} %get-tuple-element.34), channel_id=1, source_target_pairs={{1,2},{3,4},{5,6},{7,8},{9,10},{11,12},{13,14},{15,16},{17,18},{19... | collective-permute-start | bytes 393224 | tf_op jit(solution)/shard_map/ppermute | solution.py:296
  50.0 5.6 %all-gather.3 = f32[4,2,64,128]{3,2,1,0:T(8,128)S(1)} all-gather(f32[2,2,64,128]{3,2,1,0:T(8,128)S(1)} %get-tuple-element.33), channel_id=5, replica_groups={{0,1},{2,3},{4,5},{6,7},{8,9},{10,11},{12,13},{14,15},{16,17},{18,19},{..., dimensions={0}, use_global_device_ids=true | all-gather | bytes 393216 | tf_op jit(solution)/shard_map/all_gather | solution.py:298
  55.6 0.0 collective-permute-done.3.odd_ref
  55.7 0.8 %fold_columns.1 = f32[2,2,128,128]{3,2,1,0:T(8,128)} custom-call(f32[2,2,128,128]{3,2,1,0:T(8,128)S(1)} %get-tuple-element.32.own_ref, f32[2,2,2,64,128]{4,3,2,1,0:T(8,128)S(1)} %bitcast.6, f32[2,2,64,128]{3,2,1,0:T(8,128)S(1)} %collective-permute-done.3.odd_ref), custom_call_target="tpu_custom_call" | custom-call | bytes 917504 | tf_op jit(solution)/shard_map/fold_columns/pallas_call | solution.py:281
  (6 shorter events, 0.0 us)
Async XLA Ops:
  0.0 0.9 %copy-start = (f32[2,2,128,128]{3,2,1,0:T(8,128)S(1)}, f32[2,2,128,128]{3,2,1,0:T(8,128)}, u32[]{:S(2)}) copy-start(f32[2,2,128,128]{3,2,1,0:T(8,128)} %obj_ref.3) | copy-start | bytes 786436
  1.1 24.1 %collective-permute-start = (f32[2,2,64,128]{3,2,1,0:T(8,128)S(1)}, f32[2,2,64,128]{3,2,1,0:T(8,128)S(1)}, u32[]{:S(2)}, u32[]{:S(2)}) collective-permute-start(f32[2,2,64,128]{3,2,1,0:T(8,128)S(1)} %get-tuple-element.21), channel_id=1, source_target_pairs={{1,2},{3,4},{5,6},{7,8},{9,10},{11,12},{13,14},{15,16},{17,18},{19... | collective-permute-start | bytes 393224 | tf_op jit(solution)/shard_map/ppermute | solution.py:296
  25.2 9.2 %copy-start.5 = (bf16[4,256,256]{2,1,0:T(8,128)(2,1)S(1)}, bf16[4,256,256]{2,1,0:T(8,128)(2,1)}, u32[]{:S(2)}) copy-start(bf16[4,256,256]{2,1,0:T(8,128)(2,1)} %constant.2.clone.table_ref) | copy-start | bytes 1572868
  25.3 9.0 %collective-permute-start.1 = (f32[2,2,64,256]{3,2,1,0:T(8,128)S(1)}, f32[2,2,64,256]{3,2,1,0:T(8,128)S(1)}, u32[]{:S(2)}, u32[]{:S(2)}) collective-permute-start(f32[2,2,64,256]{3,2,1,0:T(8,128)S(1)} %get-tuple-element.25.own_odd_ref), channel_id=1, source_target_pairs={{64,128},{192,256},{320,384},{448,512},{576,640},{704,768},{832,89... | collective-permute-start | bytes 786440 | tf_op jit(solution)/shard_map/ppermute | solution.py:296
  28.0 2.8 %copy-start.1 = (f32[128,128]{1,0:T(8,128)S(1)}, f32[128,128]{1,0:T(8,128)}, u32[]{:S(2)}) copy-start(f32[128,128]{1,0:T(8,128)} %phase_ref) | copy-start | bytes 196612
  28.0 6.3 %copy-start.3 = (f32[2,128,128]{2,1,0:T(8,128)S(1)}, f32[2,128,128]{2,1,0:T(8,128)}, u32[]{:S(2)}) copy-start(f32[2,128,128]{2,1,0:T(8,128)} %probe_ref.1) | copy-start | bytes 393220
  28.1 6.3 %copy-start.4 = (f32[1,1,2,128,128]{4,3,2,1,0:T(8,128)S(1)}, f32[1,1,2,128,128]{4,3,2,1,0:T(8,128)}, u32[]{:S(2)}) copy-start(f32[1,1,2,128,128]{4,3,2,1,0:T(8,128)} %param.10) | copy-start | bytes 393220
  30.8 0.7 %copy-start.2 = (s32[1,1,2,2]{3,2,1,0:T(2,128)S(1)}, s32[1,1,2,2]{3,2,1,0:T(2,128)}, u32[]{:S(2)}) copy-start(s32[1,1,2,2]{3,2,1,0:T(2,128)} %positions_ref.1) | copy-start | bytes 52
  37.4 8.9 %collective-permute-start.2 = (f32[2,2,64,256]{3,2,1,0:T(8,128)S(1)}, f32[2,2,64,256]{3,2,1,0:T(8,128)S(1)}, u32[]{:S(2)}, u32[]{:S(2)}) collective-permute-start(f32[2,2,64,256]{3,2,1,0:T(8,128)S(1)} %get-tuple-element.31), channel_id=1, source_target_pairs={{64,128},{192,256},{320,384},{448,512},{576,640},{704,768},{832,89... | collective-permute-start | bytes 786440 | tf_op jit(solution)/shard_map/ppermute | solution.py:296
  46.4 9.2 %collective-permute-start.3 = (f32[2,2,64,128]{3,2,1,0:T(8,128)S(1)}, f32[2,2,64,128]{3,2,1,0:T(8,128)S(1)}, u32[]{:S(2)}, u32[]{:S(2)}) collective-permute-start(f32[2,2,64,128]{3,2,1,0:T(8,128)S(1)} %get-tuple-element.34), channel_id=1, source_target_pairs={{1,2},{3,4},{5,6},{7,8},{9,10},{11,12},{13,14},{15,16},{17,18},{19... | collective-permute-start | bytes 393224 | tf_op jit(solution)/shard_map/ppermute | solution.py:296
